TPU v7x, 256 devices: a whole 4x4x8 slice. The times are simulated.
256 devices in a mesh: dp: 32 (over y, x, core), tensor: 8 (over z).
Axes of the slice: x: 4, y: 4, z: 8, core: 2. Of those that a mesh axis runs over, the one named last changes fastest.
Arguments:
- question_vectors: bfloat16 [64, 128, 8192], P('dp', None, 'tensor'), may hold values from -112 to 112
- arriving_lookup_vectors: bfloat16 [64, 128, 1024], P('dp', None, 'tensor'), may hold values from -4 to 4
- arriving_content_vectors: bfloat16 [64, 128, 1024], P('dp', None, 'tensor'), may hold values from -24 to 24
- earlier_lookup_store: bfloat16 [128, 512, 1024], P('dp', None, 'tensor'), may hold values from -6 to 6
- earlier_content_store: bfloat16 [128, 512, 1024], P('dp', None, 'tensor'), may hold values from -24 to 24
- stored_extent: int32 [128], P('dp'), may hold values from 1 to 512
- kept_parent: int32 [64], P('dp'), may hold values from 0 to 127, as said below
- final_projection_matrix: bfloat16 [8192, 8192], P('tensor', 'dp'), may hold values from -0.0625 to 0.0625
- skip_stream: bfloat16 [8192, 8192], P('dp', 'tensor'), may hold values from -3 to 3
Outputs:
- layer_out: bfloat16 [8192, 8192], P('dp', 'tensor')
Inputs may be any that keep to these rules, and one draw needn't show every extreme that they name: `kept_parent`: no two values are equal. The 2 rows of one device continue trajectories cached on 2 different devices, and exactly 2 trajectories of each device survive.
All inputs are finite; a program needn't handle non-finite values.
Results may differ from a plain program's by a relative error of at most 0.018.
Values may be sent and summed in bfloat16 or wider, within the bound.
A program may use at most 128 MiB of HBM per device.

v0:
```python
import math

import jax
import jax.numpy as jnp
from jax import lax
from jax.sharding import PartitionSpec as P

HEAD_DIM = 128
STRETCH = 128
CACHE = 512


def attend(
    question_vectors, arriving_lookup_vectors, arriving_content_vectors, keys_in, values_in, lengths
):
    tally_lines = question_vectors.shape[0]
    groups = arriving_lookup_vectors.shape[2] // HEAD_DIM
    head_count = question_vectors.shape[2] // HEAD_DIM
    per_group = head_count // groups
    key_span = CACHE + STRETCH
    query_all = question_vectors.reshape(tally_lines, STRETCH, groups, per_group, HEAD_DIM)
    key_all = jnp.concatenate([keys_in, arriving_lookup_vectors], axis=1).reshape(
        tally_lines, key_span, groups, HEAD_DIM
    )
    value_all = jnp.concatenate([values_in, arriving_content_vectors], axis=1).reshape(
        tally_lines, key_span, groups, HEAD_DIM
    )
    scores = jnp.einsum(
        "rcgqd,rkgd->rgqck", query_all, key_all, preferred_element_type=jnp.float32
    ) / math.sqrt(HEAD_DIM)
    position = jnp.arange(key_span)
    query_pos = jnp.arange(STRETCH)
    in_cache = position[None, None, :] < lengths[:, None, None]
    in_stretch = position[None, :] - CACHE <= query_pos[:, None]
    allowed = jnp.where(position[None, None, :] < CACHE, in_cache, in_stretch[None])
    scores = jnp.where(allowed[:, None, None], scores, -jnp.inf)
    peak = jnp.max(scores, axis=-1, keepdims=True)
    raised = jnp.exp(scores - peak)
    probs = (raised / jnp.sum(raised, axis=-1, keepdims=True)).astype(jnp.bfloat16)
    mixed = jnp.einsum("rgqck,rkgd->rcgqd", probs, value_all, preferred_element_type=jnp.float32)
    return mixed.astype(jnp.bfloat16).reshape(tally_lines, STRETCH, head_count * HEAD_DIM)


def local(
    question_vectors,
    arriving_lookup_vectors,
    arriving_content_vectors,
    earlier_lookup_store,
    earlier_content_store,
    stored_extent,
    kept_parent,
    final_projection_matrix,
    skip_stream,
):
    tally_places = earlier_lookup_store.shape[0]
    tally_lines = kept_parent.shape[0]
    dp_count = lax.axis_size("dp")
    device_rank_here = lax.axis_index("dp")
    kept_parent_shared, extent_gathered_all = (
        lax.all_gather(kept_parent, "dp", axis=0, tiled=True),
        lax.all_gather(stored_extent, "dp", axis=0, tiled=True),
    )
    sender_device = kept_parent_shared // tally_places
    device_place_shared = kept_parent_shared % tally_places
    device_lines_here = lax.dynamic_slice_in_dim(
        kept_parent_shared, device_rank_here * tally_lines, tally_lines
    )
    lengths = extent_gathered_all[device_lines_here]
    from_here = (sender_device == device_rank_here).reshape(dp_count, tally_lines)
    local_slot = device_place_shared.reshape(dp_count, tally_lines)
    picked = jnp.sum(jnp.where(from_here, local_slot, 0), axis=1)
    send_keys = earlier_lookup_store[picked]
    send_values = earlier_content_store[picked]
    recv_keys, recv_values = (
        lax.all_to_all(send_keys, "dp", split_axis=0, concat_axis=0, tiled=True),
        lax.all_to_all(send_values, "dp", split_axis=0, concat_axis=0, tiled=True),
    )
    my_sources = device_lines_here // tally_places
    keys_in = recv_keys[my_sources]
    values_in = recv_values[my_sources]
    attended = attend(
        question_vectors,
        arriving_lookup_vectors,
        arriving_content_vectors,
        keys_in,
        values_in,
        lengths,
    )
    flat = attended.reshape(tally_lines * STRETCH, attended.shape[2])
    terms = jnp.dot(
        flat,
        lax.all_gather(final_projection_matrix, "dp", axis=1, tiled=True),
        preferred_element_type=jnp.float32,
    )
    summed = lax.psum_scatter(
        terms.astype(jnp.bfloat16), "tensor", scatter_dimension=1, tiled=True
    ).astype(jnp.float32)
    return (skip_stream.astype(jnp.float32) + summed).astype(jnp.bfloat16)


def solution(mesh):
    return jax.shard_map(
        local,
        mesh=mesh,
        in_specs=(
            P("dp", None, "tensor"),
            P("dp", None, "tensor"),
            P("dp", None, "tensor"),
            P("dp", None, "tensor"),
            P("dp", None, "tensor"),
            P("dp"),
            P("dp"),
            P("tensor", "dp"),
            P("dp", "tensor"),
        ),
        out_specs=P("dp", "tensor"),
        check_vma=False,
    )
```

profile of v0, /device:TPU:1, one launch (start us, length us, event | category | flops | bytes accessed | tf_op | source)
XLA Modules:
  0.0 255.4 jit_solution(10917257285820550618)
XLA Ops:
  6.5 0.7 all-gather.2.cloned.1.call-update
  7.3 1.3 dynamic-slice
  9.8 0.9 dynamic-update-slice
  10.7 0.8 dynamic-update-slice.1
  11.5 14.4 %all-reduce.2 = (s32[64]{0:T(128)S(1)}, s32[128]{0:T(128)S(1)}) all-reduce(s32[64]{0:T(128)S(1)} %dynamic-update-slice, s32[128]{0:T(128)S(1)} %dynamic-update-slice.1), channel_id=1, replica_groups=mesh['dp'=32,'tensor'=8] {'dp'}, use_global_device_ids=true, to_apply=%add | all-reduce | flops 192 | bytes 1536
  26.0 0.1 select_n.60
  26.1 0.1 reduce_sum.20
  26.3 3.0 %gather_fusion = bf16[32,512,128]{2,1,0:T(8,128)(2,1)} fusion(bf16[4,512,128]{2,1,0:T(8,128)(2,1)S(1)} %copy-done, s32[1024]{0:T(1024)S(1)} %pad_clamp_fusion.2), kind=kCustom, calls=%fused_computation | custom fusion | bytes 8388736 | tf_op jit(solution)/shard_map/gather | solution.py:73
  29.3 8.5 %all-to-all-start = ((bf16[32,512,128]{2,1,0:T(8,128)(2,1)}), bf16[32,512,128]{2,1,0:T(8,128)(2,1)}, u32[]{:S(2)}, u32[]{:S(2)}) async-start(bf16[32,512,128]{2,1,0:T(8,128)(2,1)} %gather_fusion), calls=%async_computation | async-start | bytes 8388608 | tf_op jit(solution)/shard_map/all_to_all | solution.py:76
  37.8 3.0 %gather_fusion.3 = bf16[32,512,128]{2,1,0:T(8,128)(2,1)} fusion(bf16[4,512,128]{2,1,0:T(8,128)(2,1)S(1)} %copy-done.1, s32[1024]{0:T(1024)S(1)} %pad_clamp_fusion.2), kind=kCustom, calls=%fused_computation.3 | custom fusion | bytes 8388736 | tf_op jit(solution)/shard_map/gather | solution.py:72
  40.9 53.6 %all-to-all-done = bf16[32,512,128]{2,1,0:T(8,128)(2,1)} async-done(((bf16[32,512,128]{2,1,0:T(8,128)(2,1)}), bf16[32,512,128]{2,1,0:T(8,128)(2,1)}, u32[]{:S(2)}, u32[]{:S(2)}) %all-to-all-start) | async-done | bytes 4194336 | tf_op jit(solution)/shard_map/all_to_all | solution.py:76
  94.5 12.5 %all-to-all-start.1 = ((bf16[32,512,128]{2,1,0:T(8,128)(2,1)}), bf16[32,512,128]{2,1,0:T(8,128)(2,1)}, u32[]{:S(2)}, u32[]{:S(2)}) async-start(bf16[32,512,128]{2,1,0:T(8,128)(2,1)} %gather_fusion.3), calls=%async_computation.1 | async-start | bytes 8388608 | tf_op jit(solution)/shard_map/all_to_all | solution.py:75
  107.0 0.0 reduce-scatter.2.cloned.1.call-start
  107.0 0.1 copy.14
  107.2 0.1 compare_select_fusion.3
  107.3 0.6 gather_fusion.2
  107.9 0.1 iota_compare_fusion.1
  108.0 0.2 iota_compare_fusion
  108.1 0.3 broadcast_select_fusion
  108.5 2.8 %gather_fusion.1 = bf16[2,512,128]{2,1,0:T(8,128)(2,1)S(1)} fusion(bf16[32,512,128]{2,1,0:T(8,128)(2,1)} %all-to-all-done, s32[1024]{0:T(1024)S(1)} %pad_clamp_fusion.1), kind=kCustom, calls=%fused_computation.1 | custom fusion | bytes 524296 | tf_op jit(solution)/shard_map/gather | solution.py:80
  111.3 0.1 copy.13
  111.4 60.9 %all-to-all-done.1 = bf16[32,512,128]{2,1,0:T(8,128)(2,1)} async-done(((bf16[32,512,128]{2,1,0:T(8,128)(2,1)}), bf16[32,512,128]{2,1,0:T(8,128)(2,1)}, u32[]{:S(2)}, u32[]{:S(2)}) %all-to-all-start.1) | async-done | bytes 4194336 | tf_op jit(solution)/shard_map/all_to_all | solution.py:75
  172.3 2.8 %gather_fusion.4 = bf16[2,512,128]{2,1,0:T(8,128)(2,1)S(1)} fusion(bf16[32,512,128]{2,1,0:T(8,128)(2,1)} %all-to-all-done.1, s32[1024]{0:T(1024)S(1)} %pad_clamp_fusion.1), kind=kCustom, calls=%fused_computation.4 | custom fusion | bytes 524296 | tf_op jit(solution)/shard_map/gather | solution.py:79
  175.1 0.9 fusion.1
  176.0 1.1 fusion
  177.1 1.6 fusion.8
  178.7 0.3 copy.17
  179.0 0.0 all-gather.2.cloned.1.call-done
  179.1 11.9 %convolution_convert_fusion = bf16[256,8192]{1,0:T(8,128)(2,1)} fusion(bf16[1024,8192]{1,0:T(8,128)(2,1)} %all-gather.2.cloned.1.call-done, bf16[32,8,8,128]{3,2,1,0:T(8,128)(2,1)S(1)} %bitcast.62), kind=kOutput, calls=%fused_computation.5 | convolution fusion | flops 4297064448 | bytes 21495808 | tf_op jit(solution)/shard_map/dot_general | solution.py:90
  190.9 0.0 reduce-scatter.2.cloned.1.call-update
  190.9 55.6 %reduce-scatter.2.cloned.1.call-done = bf16[256,1024]{1,0:T(8,128)(2,1)} async-done(((bf16[256,8192]{1,0:T(8,128)(2,1)}), bf16[256,1024]{1,0:T(8,128)(2,1)}) %reduce-scatter.2.cloned.1.call-update) | async-done | bytes 524304 | tf_op jit(solution)/shard_map/reduce_scatter | solution.py:95
  246.5 2.0 add_convert_fusion
  (22 shorter events, 0.1 us)
Async XLA Ops:
  6.5 19.7 %copy-start = (bf16[4,512,128]{2,1,0:T(8,128)(2,1)S(1)}, bf16[4,512,128]{2,1,0:T(8,128)(2,1)}, u32[]{:S(2)}) copy-start(bf16[4,512,128]{2,1,0:T(8,128)(2,1)} %param.13) | copy-start | bytes 1572868
  6.5 172.5 %all-gather.2.cloned.1.call-start = ((), (), s32[]{:S(2)}) async-start(), calls=%async_computation.3 | async-start | bytes 17301504 | tf_op jit(solution)/shard_map/all_gather | solution.py:92
  29.3 8.6 %copy-start.1 = (bf16[4,512,128]{2,1,0:T(8,128)(2,1)S(1)}, bf16[4,512,128]{2,1,0:T(8,128)(2,1)}, u32[]{:S(2)}) copy-start(bf16[4,512,128]{2,1,0:T(8,128)(2,1)} %param.12) | copy-start | bytes 1572868
  29.3 65.2 %all-to-all-start = ((bf16[32,512,128]{2,1,0:T(8,128)(2,1)}), bf16[32,512,128]{2,1,0:T(8,128)(2,1)}, u32[]{:S(2)}, u32[]{:S(2)}) async-start(bf16[32,512,128]{2,1,0:T(8,128)(2,1)} %gather_fusion), calls=%async_computation | async-start | bytes 8388608 | tf_op jit(solution)/shard_map/all_to_all | solution.py:76
  40.9 66.1 %copy-start.3 = (bf16[2,128,128]{2,1,0:T(8,128)(2,1)S(1)}, bf16[2,128,128]{2,1,0:T(8,128)(2,1)}, u32[]{:S(2)}) copy-start(bf16[2,128,128]{2,1,0:T(8,128)(2,1)} %param.11) | copy-start | bytes 196612
  40.9 134.2 %copy-start.4 = (bf16[2,128,1024]{2,1,0:T(8,128)(2,1)S(1)}, bf16[2,128,1024]{2,1,0:T(8,128)(2,1)}, u32[]{:S(2)}) copy-start(bf16[2,128,1024]{2,1,0:T(8,128)(2,1)} %param.9) | copy-start | bytes 1572868
  40.9 134.2 %copy-start.5 = (bf16[2,128,128]{2,1,0:T(8,128)(2,1)S(1)}, bf16[2,128,128]{2,1,0:T(8,128)(2,1)}, u32[]{:S(2)}) copy-start(bf16[2,128,128]{2,1,0:T(8,128)(2,1)} %param.10) | copy-start | bytes 196612
  94.5 77.8 %all-to-all-start.1 = ((bf16[32,512,128]{2,1,0:T(8,128)(2,1)}), bf16[32,512,128]{2,1,0:T(8,128)(2,1)}, u32[]{:S(2)}, u32[]{:S(2)}) async-start(bf16[32,512,128]{2,1,0:T(8,128)(2,1)} %gather_fusion.3), calls=%async_computation.1 | async-start | bytes 8388608 | tf_op jit(solution)/shard_map/all_to_all | solution.py:75
  107.0 139.6 %reduce-scatter.2.cloned.1.call-start = ((), (), s32[]{:S(2)}) async-start(), calls=%async_computation.4 | async-start | bytes 4718592 | tf_op jit(solution)/shard_map/reduce_scatter | solution.py:95
  179.0 67.5 %copy-start.2 = (bf16[256,1024]{1,0:T(8,128)(2,1)S(1)}, bf16[256,1024]{1,0:T(8,128)(2,1)}, u32[]{:S(2)}) copy-start(bf16[256,1024]{1,0:T(8,128)(2,1)} %param.17) | copy-start | bytes 1572868
Sparse Core Ops, SparseCore 0:
  9.8 164.6 all-gather.1
  191.1 55.4 reduce-scatter.1
where the time goes:
time: 256 us; the launch traced here: 255 us
  waiting for transfers between devices  171 us (67%)
  starting transfers between devices  21.1 us (8%)
  local copies, waits for them, and re-layouts  15.9 us (6%)
  between operations  14.9 us (6%)
  blocking collectives  14.4 us (6%)
  matrix products  14.3 us (6%)
  other arithmetic  3.91 us (2%)
    all_to_all x1, waiting for transfers between devices, local(): lax.all_to_all(send_keys, 'dp', split_axis=0, concat_axis=0, tiled=True)  60.9 us
    reduce_scatter x1, waiting for transfers between devices, local(): lax.psum_scatter(terms.astype(jnp.bfloat16), 'tensor', scatter_dimension=...  55.6 us
    all_to_all x1, waiting for transfers between devices, local(): lax.all_to_all(send_values, 'dp', split_axis=0, concat_axis=0, tiled=True)  53.6 us
    unnamed x1, blocking collectives  14.4 us
    all_to_all x1, starting transfers between devices, local(): lax.all_to_all(send_keys, 'dp', split_axis=0, concat_axis=0, tiled=True)  12.5 us
    dot_general x1, matrix products, local(): jnp.dot(flat, lax.all_gather(final_projection_matrix, 'dp', axis=1, tiled...  11.9 us
    all_to_all x1, starting transfers between devices, local(): lax.all_to_all(send_values, 'dp', split_axis=0, concat_axis=0, tiled=True)  8.54 us
  transfers between devices with their start and end apart: 4, of which 3 were waited for; matrix products, arithmetic and copies ran while one was open for 8% of the time, Pallas kernels for 0%

commit v1 on v0

--- a/solution.py
+++ b/solution.py
@@ -3,11 +3,317 @@
 import jax
 import jax.numpy as jnp
 from jax import lax
+from jax.experimental import pallas as pl
+from jax.experimental.pallas import tpu as pltpu
 from jax.sharding import PartitionSpec as P
 
 HEAD_DIM = 128
 STRETCH = 128
 CACHE = 512
+
+
+MESH = pl.DeviceIdType.MESH
+
+
+def field(word, index):
+    return jnp.bitwise_and(jnp.right_shift(jnp.int32(word), 2 * index), 3)
+
+
+def packed(values):
+    word = 0
+    for place, value in enumerate(values):
+        word |= value << (2 * place)
+    if word >= 1 << 31:
+        word -= 1 << 32
+    return word
+
+
+ORDER = [
+    (0, 0), (1, 0), (3, 0), (0, 1), (0, 3), (1, 1), (1, 3), (3, 1), (3, 3),
+    (2, 0), (0, 2), (2, 1), (2, 3), (1, 2), (3, 2), (2, 2),
+]
+EVENTS = [
+    (0, 1, 0), (0, 3, 0), (1, 0, 1), (1, 0, 3), (1, 1, 0), (1, 3, 0), (0, 0, 1), (0, 0, 3),
+    (0, 1, 1), (1, 1, 1), (0, 1, 3), (1, 1, 3), (0, 3, 1), (1, 3, 1), (0, 3, 3), (1, 3, 3),
+    (0, 2, 0), (1, 0, 2), (1, 2, 0), (0, 0, 2), (0, 2, 1), (1, 2, 1), (0, 2, 3), (1, 2, 3),
+    (1, 1, 2), (0, 1, 2), (1, 3, 2), (0, 3, 2), (0, 2, 2), (1, 2, 2),
+]
+ORDER_X = packed([o[0] for o in ORDER])
+ORDER_Y = packed([o[1] for o in ORDER])
+EVENT_TABLES = [
+    (packed([e[k] for e in EVENTS[:15]]), packed([e[k] for e in EVENTS[15:]])) for k in range(3)
+]
+
+
+def event_field(k, index):
+    low, high = EVENT_TABLES[k]
+    return jnp.where(
+        index < 15, field(low, jnp.minimum(index, 14)), field(high, jnp.maximum(index - 15, 0))
+    )
+
+
+UNITS = 32
+
+
+def project_kernel(
+    a_ref, w_ref, skip_ref, out_ref,
+    a_buf, w_buf, p_buf, r_buf, x_buf,
+    wrecv, wsend, rsem, ssem, asem, xsend, xrecv,
+):
+    dp = lax.axis_index("dp")
+    z = lax.axis_index("tensor")
+    core = lax.rem(dp, 2)
+    chip = dp // 2
+    x = lax.rem(chip, 4)
+    y = chip // 4
+
+    def dp_of(cx, cy, cc):
+        return (lax.rem(cy + 4, 4) * 4 + lax.rem(cx + 4, 4)) * 2 + cc
+
+    partner = (dp + 1 - 2 * core, z)
+
+    def plane(axis, step):
+        if isinstance(axis, int):
+            return (dp_of(x + step, y, core) if axis == 0 else dp_of(x, y + step, core), z)
+        return (
+            dp_of(x + jnp.where(axis == 0, step, 0), y + jnp.where(axis == 0, 0, step), core),
+            z,
+        )
+
+    barrier = pltpu.get_barrier_semaphore()
+    around = [partner] + [plane(axis, step) for axis in (0, 1) for step in (1, 3)]
+    around += [(dp, lax.rem(z + 1, 8)), (dp, lax.rem(z + 7, 8))]
+    for other in around:
+        pl.semaphore_signal(barrier, inc=1, device_id=other, device_id_type=MESH)
+    pl.semaphore_wait(barrier, len(around))
+
+    mine = [
+        pltpu.make_async_remote_copy(
+            src_ref=a_ref.at[pl.ds(u * 128, 128)],
+            dst_ref=a_buf.at[u, pl.ds(pl.multiple_of(core * 128, 128), 128)],
+            send_sem=asem.at[u],
+            recv_sem=asem.at[2 + u],
+            device_id=partner,
+            device_id_type=MESH,
+        )
+        for u in range(2)
+    ]
+    for copy in mine:
+        copy.start()
+
+    own = y * 4 + x
+
+    def send_half(src, block, half, axis, step):
+        rows = pl.ds(pl.multiple_of(half * 512, 512), 512)
+        pltpu.make_async_remote_copy(
+            src_ref=src.at[rows],
+            dst_ref=w_buf.at[block, rows],
+            send_sem=wsend.at[axis, step // 2],
+            recv_sem=wrecv.at[block, half],
+            device_id=plane(axis, step),
+            device_id_type=MESH,
+        ).start()
+
+    def send_quarter(block, half, axis, way):
+        rows = pl.ds(pl.multiple_of(half * 512 + way * 256, 256), 256)
+        pltpu.make_async_remote_copy(
+            src_ref=w_buf.at[block, rows],
+            dst_ref=w_buf.at[block, rows],
+            send_sem=wsend.at[axis, way],
+            recv_sem=wrecv.at[block, half],
+            device_id=plane(axis, 1 + 2 * way),
+            device_id_type=MESH,
+        ).start()
+
+    for phase in range(2):
+        for half in range(2):
+            for step in (1, 3):
+                send_half(w_ref, own, half, half ^ phase, step)
+
+    for u in range(2):
+        a_buf[u, pl.ds(pl.multiple_of(core * 128, 128), 128), :] = a_ref[pl.ds(u * 128, 128), :]
+    pltpu.make_async_copy(w_ref, w_buf.at[own], asem.at[4]).start()
+
+    def block_at(dx, dy):
+        bx = lax.rem(x - dx + 4, 4)
+        by = lax.rem(y - dy + 4, 4)
+        return bx, by, by * 4 + bx
+
+    def arrival(event, carry):
+        half = event_field(0, event)
+        dx = event_field(1, event)
+        dy = event_field(2, event)
+        _, _, block = block_at(dx, dy)
+        rows = pl.ds(pl.multiple_of(half * 512, 512), 512)
+        landed = w_buf.at[block, rows]
+        pltpu.make_async_copy(landed, landed, wrecv.at[block, half]).wait()
+        near = jnp.where(half == 0, dx, dy)
+        far = jnp.where(half == 0, dy, dx)
+        second = 1 - half
+
+        @pl.when(far == 0)
+        def _():
+            for step in (1, 3):
+                send_half(w_buf.at[block], block, half, second, step)
+
+        @pl.when((far == 0) & ((near == 1) | (near == 3)))
+        def _():
+            send_quarter(block, half, half, near // 2)
+
+        @pl.when((far == 1) | (far == 3))
+        def _():
+            send_quarter(block, half, second, far // 2)
+
+        return carry
+
+    def events_by(i):
+        return jnp.where(i < 1, 0, jnp.minimum(jnp.maximum(jnp.minimum(i + 3, 22), i), 30))
+
+    def chain(i, lag, h):
+        unit = i - 2 * lag
+        stage = jnp.clip(unit // 2, 0, 15)
+        u = lax.rem(unit + 64, 2)
+        bx, by, _ = block_at(field(ORDER_X, stage), field(ORDER_Y, stage))
+        goal = 2 * by + bx // 2
+        d = lax.rem(goal - z + 8, 8)
+        live = (unit >= 0) & (unit < UNITS)
+        slot = jnp.clip(unit, 0, UNITS - 1)
+        rows = pl.ds(h * 128, 128)
+        if lag < 4:
+            reach = 4 if h == 0 else 3
+            down = jnp.where(d > reach, 1, 0)
+            level = jnp.where(d > reach, d - reach - 1, reach - d)
+
+            @pl.when(live & (d > 0) & (level == lag))
+            def _():
+                if lag > 0:
+                    landed = r_buf.at[down, slot, rows]
+                    pltpu.make_async_copy(landed, landed, rsem.at[down, slot, h]).wait()
+                    p_buf[slot, rows, :] = (
+                        p_buf[slot, rows, :].astype(jnp.float32)
+                        + r_buf[down, slot, rows, :].astype(jnp.float32)
+                    ).astype(jnp.bfloat16)
+                pltpu.make_async_remote_copy(
+                    src_ref=p_buf.at[slot, rows],
+                    dst_ref=r_buf.at[down, slot, rows],
+                    send_sem=ssem,
+                    recv_sem=rsem.at[down, slot, h],
+                    device_id=(dp, lax.rem(z + 1 + 6 * down, 8)),
+                    device_id_type=MESH,
+                ).start()
+        else:
+            k = lax.rem(bx, 2)
+
+            @pl.when(live & (d == 0))
+            def _():
+                for way in range(2):
+                    landed = r_buf.at[way, slot, rows]
+                    pltpu.make_async_copy(landed, landed, rsem.at[way, slot, h]).wait()
+                total = (
+                    p_buf[slot, rows, :].astype(jnp.float32)
+                    + r_buf[0, slot, rows, :].astype(jnp.float32)
+                    + r_buf[1, slot, rows, :].astype(jnp.float32)
+                )
+
+                @pl.when(core == h)
+                def _():
+                    tokens = pl.ds(pl.multiple_of(u * 128, 128), 128)
+                    columns = pl.ds(pl.multiple_of((2 * k + core) * 256, 256), 256)
+                    out_ref[tokens, columns] = (
+                        skip_ref[tokens, columns].astype(jnp.float32) + total
+                    ).astype(jnp.bfloat16)
+
+                @pl.when(core != h)
+                def _():
+                    p_buf[slot, rows, :] = total.astype(jnp.bfloat16)
+                    pltpu.make_async_remote_copy(
+                        src_ref=p_buf.at[slot, rows],
+                        dst_ref=x_buf.at[k, u],
+                        send_sem=xsend.at[k, u],
+                        recv_sem=xrecv.at[k, u],
+                        device_id=partner,
+                        device_id_type=MESH,
+                    ).start()
+
+    def unit_step(i, carry):
+        lax.fori_loop(events_by(i - 1), events_by(i), arrival, 0)
+
+        @pl.when(i == 0)
+        def _():
+            pltpu.make_async_copy(w_ref, w_buf.at[own], asem.at[4]).wait()
+
+        @pl.when(i < 2)
+        def _():
+            u = jnp.clip(i, 0, 1)
+            landed = a_buf.at[u, pl.ds(pl.multiple_of((1 - core) * 128, 128), 128)]
+            pltpu.make_async_copy(landed, landed, asem.at[2 + u]).wait()
+
+        @pl.when(i < UNITS)
+        def _():
+            stage = jnp.clip(i // 2, 0, 15)
+            _, _, block = block_at(field(ORDER_X, stage), field(ORDER_Y, stage))
+            p_buf[jnp.clip(i, 0, UNITS - 1)] = jnp.dot(
+                a_buf[lax.rem(i, 2)], w_buf[block], preferred_element_type=jnp.float32
+            ).astype(jnp.bfloat16)
+
+        for lag in range(5):
+            for h in range(2):
+                chain(i, lag, h)
+        return carry
+
+    lax.fori_loop(0, UNITS + 8, unit_step, 0)
+
+    for k in range(2):
+        for u in range(2):
+            landed = x_buf.at[k, u]
+            pltpu.make_async_copy(landed, landed, xrecv.at[k, u]).wait()
+            tokens = pl.ds(u * 128, 128)
+            columns = pl.ds(pl.multiple_of((2 * k + 1 - core) * 256, 256), 256)
+            out_ref[tokens, columns] = (
+                skip_ref[tokens, columns].astype(jnp.float32) + x_buf[k, u].astype(jnp.float32)
+            ).astype(jnp.bfloat16)
+
+    for u in range(2):
+        mine[u].wait_send()
+        for k in range(2):
+            landed = x_buf.at[k, u]
+            pltpu.make_async_copy(landed, landed, xsend.at[k, u]).wait()
+    for axis in range(2):
+        for way in range(2):
+            sent = w_buf.at[pl.ds(0, 15), pl.ds(0, 256)]
+            pltpu.make_async_copy(sent, sent, wsend.at[axis, way]).wait()
+    sent = p_buf.at[pl.ds(0, 28)]
+    pltpu.make_async_copy(sent, sent, ssem).wait()
+
+
+def project(flat, weights, skip):
+    vmem = pl.BlockSpec(memory_space=pltpu.VMEM)
+    return pl.pallas_call(
+        project_kernel,
+        out_shape=jax.ShapeDtypeStruct(skip.shape, skip.dtype),
+        in_specs=[vmem, vmem, vmem],
+        out_specs=vmem,
+        scratch_shapes=[
+            pltpu.VMEM((2, 256, 1024), jnp.bfloat16),
+            pltpu.VMEM((16, 1024, 256), jnp.bfloat16),
+            pltpu.VMEM((UNITS, 256, 256), jnp.bfloat16),
+            pltpu.VMEM((2, UNITS, 256, 256), jnp.bfloat16),
+            pltpu.VMEM((2, 2, 128, 256), jnp.bfloat16),
+            pltpu.SemaphoreType.DMA((16, 2)),
+            pltpu.SemaphoreType.DMA((2, 2)),
+            pltpu.SemaphoreType.DMA((2, UNITS, 2)),
+            pltpu.SemaphoreType.DMA,
+            pltpu.SemaphoreType.DMA((5,)),
+            pltpu.SemaphoreType.DMA((2, 2)),
+            pltpu.SemaphoreType.DMA((2, 2)),
+        ],
+        compiler_params=pltpu.CompilerParams(
+            collective_id=1, has_side_effects=True, vmem_limit_bytes=48 * 1024 * 1024
+        ),
+        cost_estimate=pl.CostEstimate(
+            flops=2 * 512 * 1024 * 4096, bytes_accessed=16 << 20, transcendentals=0
+        ),
+    )(flat, weights, skip)
 
 
 def attend(
@@ -87,15 +393,7 @@
         lengths,
     )
     flat = attended.reshape(tally_lines * STRETCH, attended.shape[2])
-    terms = jnp.dot(
-        flat,
-        lax.all_gather(final_projection_matrix, "dp", axis=1, tiled=True),
-        preferred_element_type=jnp.float32,
-    )
-    summed = lax.psum_scatter(
-        terms.astype(jnp.bfloat16), "tensor", scatter_dimension=1, tiled=True
-    ).astype(jnp.float32)
-    return (skip_stream.astype(jnp.float32) + summed).astype(jnp.bfloat16)
+    return project(flat, final_projection_matrix, skip_stream)
 
 
 def solution(mesh):

time: 256 us -> 253 us (0.988)
  the two profiles are of different devices: /device:TPU:1 before, /device:TPU:23 now
where the time goes in v1:
time: 253 us
  Pallas kernels  108 us (43%)
  waiting for transfers between devices  90.1 us (36%)
  starting transfers between devices  22.6 us (9%)
  local copies, waits for them, and re-layouts  16.9 us (7%)
  blocking collectives  9.07 us (4%)
    pallas_call x1, Pallas kernels, project(): pl.pallas_call(project_kernel, out_shape=jax.ShapeDtypeStruct(skip.shape,...  108 us
    all_to_all x1, waiting for transfers between devices, local(): lax.all_to_all(send_values, 'dp', split_axis=0, concat_axis=0, tiled=True)  45.7 us
    all_to_all x1, waiting for transfers between devices, local(): lax.all_to_all(send_keys, 'dp', split_axis=0, concat_axis=0, tiled=True)  44.4 us
    all_to_all x1, starting transfers between devices, local(): lax.all_to_all(send_values, 'dp', split_axis=0, concat_axis=0, tiled=True)  13.1 us
    all_to_all x1, starting transfers between devices, local(): lax.all_to_all(send_keys, 'dp', split_axis=0, concat_axis=0, tiled=True)  9.54 us
    unnamed x1, blocking collectives  9.07 us
  transfers between devices with their start and end apart: 2, of which 2 were waited for; matrix products, arithmetic and copies ran while one was open for 3% of the time, Pallas kernels for 0%

profile of v1, /device:TPU:23, one launch (start us, length us, event | category | flops | bytes accessed | tf_op | source)
XLA Modules:
  0.0 252.7 jit_solution(10992390091396890175)
XLA Ops:
  0.0 1.3 dynamic-slice
  2.6 0.9 dynamic-update-slice
  3.5 0.8 dynamic-update-slice.1
  4.3 9.1 %all-reduce.2 = (s32[64]{0:T(128)S(1)}, s32[128]{0:T(128)S(1)}) all-reduce(s32[64]{0:T(128)S(1)} %dynamic-update-slice, s32[128]{0:T(128)S(1)} %dynamic-update-slice.1), channel_id=1, replica_groups=mesh['dp'=32,'tensor'=8] {'dp'}, use_global_device_ids=true, to_apply=%add | all-reduce | flops 192 | bytes 1536
  13.4 0.1 select_n.60
  13.5 0.1 reduce_sum.20
  13.7 3.0 %gather_fusion = bf16[32,512,128]{2,1,0:T(8,128)(2,1)} fusion(bf16[4,512,128]{2,1,0:T(8,128)(2,1)S(1)} %copy-done, s32[1024]{0:T(1024)S(1)} %pad_clamp_fusion.2), kind=kCustom, calls=%fused_computation | custom fusion | bytes 8388736 | tf_op jit(solution)/shard_map/gather | solution.py:379
  16.7 13.1 %all-to-all-start = ((bf16[32,512,128]{2,1,0:T(8,128)(2,1)}), bf16[32,512,128]{2,1,0:T(8,128)(2,1)}, u32[]{:S(2)}, u32[]{:S(2)}) async-start(bf16[32,512,128]{2,1,0:T(8,128)(2,1)} %gather_fusion), calls=%async_computation | async-start | bytes 8388608 | tf_op jit(solution)/shard_map/all_to_all | solution.py:382
  29.8 3.1 %gather_fusion.3 = bf16[32,512,128]{2,1,0:T(8,128)(2,1)} fusion(bf16[4,512,128]{2,1,0:T(8,128)(2,1)S(1)} %copy-done.3, s32[1024]{0:T(1024)S(1)} %pad_clamp_fusion.2), kind=kCustom, calls=%fused_computation.3 | custom fusion | bytes 8388736 | tf_op jit(solution)/shard_map/gather | solution.py:378
  32.9 45.7 %all-to-all-done = bf16[32,512,128]{2,1,0:T(8,128)(2,1)} async-done(((bf16[32,512,128]{2,1,0:T(8,128)(2,1)}), bf16[32,512,128]{2,1,0:T(8,128)(2,1)}, u32[]{:S(2)}, u32[]{:S(2)}) %all-to-all-start) | async-done | bytes 4194336 | tf_op jit(solution)/shard_map/all_to_all | solution.py:382
  78.6 9.5 %all-to-all-start.1 = ((bf16[32,512,128]{2,1,0:T(8,128)(2,1)}), bf16[32,512,128]{2,1,0:T(8,128)(2,1)}, u32[]{:S(2)}, u32[]{:S(2)}) async-start(bf16[32,512,128]{2,1,0:T(8,128)(2,1)} %gather_fusion.3), calls=%async_computation.1 | async-start | bytes 8388608 | tf_op jit(solution)/shard_map/all_to_all | solution.py:381
  88.2 0.1 copy.15
  88.3 0.1 compare_select_fusion.3
  88.4 0.6 gather_fusion.2
  89.1 0.1 iota_compare_fusion.1
  89.2 0.2 iota_compare_fusion
  89.3 0.3 broadcast_select_fusion
  89.6 2.8 %gather_fusion.1 = bf16[2,512,128]{2,1,0:T(8,128)(2,1)S(1)} fusion(bf16[32,512,128]{2,1,0:T(8,128)(2,1)} %all-to-all-done, s32[1024]{0:T(1024)S(1)} %pad_clamp_fusion.1), kind=kCustom, calls=%fused_computation.1 | custom fusion | bytes 524296 | tf_op jit(solution)/shard_map/gather | solution.py:386
  92.4 0.1 copy.14
  92.6 44.4 %all-to-all-done.1 = bf16[32,512,128]{2,1,0:T(8,128)(2,1)} async-done(((bf16[32,512,128]{2,1,0:T(8,128)(2,1)}), bf16[32,512,128]{2,1,0:T(8,128)(2,1)}, u32[]{:S(2)}, u32[]{:S(2)}) %all-to-all-start.1) | async-done | bytes 4194336 | tf_op jit(solution)/shard_map/all_to_all | solution.py:381
  137.0 2.8 %gather_fusion.4 = bf16[2,512,128]{2,1,0:T(8,128)(2,1)S(1)} fusion(bf16[32,512,128]{2,1,0:T(8,128)(2,1)} %all-to-all-done.1, s32[1024]{0:T(1024)S(1)} %pad_clamp_fusion.1), kind=kCustom, calls=%fused_computation.4 | custom fusion | bytes 524296 | tf_op jit(solution)/shard_map/gather | solution.py:385
  139.8 0.0 copy-done.5
  139.8 0.0 copy-done.6
  139.8 0.9 fusion.1
  140.7 1.1 fusion
  141.8 0.0 copy-start.1
  141.8 0.0 copy-start.2
  141.8 1.6 fusion.8
  143.4 0.3 copy.18
  143.7 0.1 copy.31
  143.8 108.0 %shard_map.91 = bf16[256,1024]{1,0:T(8,128)(2,1)S(1)} custom-call(bf16[256,1024]{1,0:T(8,128)(2,1)S(1)} %bitcast.61, bf16[1024,256]{1,0:T(8,128)(2,1)S(1)} %copy-done.1, bf16[256,1024]{1,0:T(8,128)(2,1)S(1)} %copy-done.2), custom_call_target="tpu_custom_call" | custom-call | flops 4294967296 | bytes 16777216 | tf_op jit(solution)/shard_map/pallas_call | solution.py:291
  251.9 0.8 copy.35
  (19 shorter events, 0.1 us)
Async XLA Ops:
  0.0 13.7 %copy-start = (bf16[4,512,128]{2,1,0:T(8,128)(2,1)S(1)}, bf16[4,512,128]{2,1,0:T(8,128)(2,1)}, u32[]{:S(2)}) copy-start(bf16[4,512,128]{2,1,0:T(8,128)(2,1)} %param.13) | copy-start | bytes 1572868
  16.7 13.1 %copy-start.3 = (bf16[4,512,128]{2,1,0:T(8,128)(2,1)S(1)}, bf16[4,512,128]{2,1,0:T(8,128)(2,1)}, u32[]{:S(2)}) copy-start(bf16[4,512,128]{2,1,0:T(8,128)(2,1)} %param.12) | copy-start | bytes 1572868
  16.7 61.9 %all-to-all-start = ((bf16[32,512,128]{2,1,0:T(8,128)(2,1)}), bf16[32,512,128]{2,1,0:T(8,128)(2,1)}, u32[]{:S(2)}, u32[]{:S(2)}) async-start(bf16[32,512,128]{2,1,0:T(8,128)(2,1)} %gather_fusion), calls=%async_computation | async-start | bytes 8388608 | tf_op jit(solution)/shard_map/all_to_all | solution.py:382
  32.9 55.3 %copy-start.4 = (bf16[2,128,128]{2,1,0:T(8,128)(2,1)S(1)}, bf16[2,128,128]{2,1,0:T(8,128)(2,1)}, u32[]{:S(2)}) copy-start(bf16[2,128,128]{2,1,0:T(8,128)(2,1)} %param.11) | copy-start | bytes 196612
  32.9 106.9 %copy-start.5 = (bf16[2,128,1024]{2,1,0:T(8,128)(2,1)S(1)}, bf16[2,128,1024]{2,1,0:T(8,128)(2,1)}, u32[]{:S(2)}) copy-start(bf16[2,128,1024]{2,1,0:T(8,128)(2,1)} %param.9) | copy-start | bytes 1572868
  32.9 106.9 %copy-start.6 = (bf16[2,128,128]{2,1,0:T(8,128)(2,1)S(1)}, bf16[2,128,128]{2,1,0:T(8,128)(2,1)}, u32[]{:S(2)}) copy-start(bf16[2,128,128]{2,1,0:T(8,128)(2,1)} %param.10) | copy-start | bytes 196612
  78.6 58.4 %all-to-all-start.1 = ((bf16[32,512,128]{2,1,0:T(8,128)(2,1)}), bf16[32,512,128]{2,1,0:T(8,128)(2,1)}, u32[]{:S(2)}, u32[]{:S(2)}) async-start(bf16[32,512,128]{2,1,0:T(8,128)(2,1)} %gather_fusion.3), calls=%async_computation.1 | async-start | bytes 8388608 | tf_op jit(solution)/shard_map/all_to_all | solution.py:381
  141.8 2.0 copy-start.1
  141.8 2.0 copy-start.2

commit v2 on v1

--- a/solution.py
+++ b/solution.py
@@ -314,6 +314,284 @@
             flops=2 * 512 * 1024 * 4096, bytes_accessed=16 << 20, transcendentals=0
         ),
     )(flat, weights, skip)
+
+
+def spots():
+    dp = lax.axis_index("dp")
+    core = lax.rem(dp, 2)
+    chip = dp // 2
+    return dp, lax.axis_index("tensor"), core, lax.rem(chip, 4), chip // 4
+
+
+def table_kernel(mine_ref, out_ref, landing, send_sem, recv_sem):
+    dp, z, _, _, _ = spots()
+    barrier = pltpu.get_barrier_semaphore()
+
+    def greet(step, carry):
+        pl.semaphore_signal(
+            barrier, inc=1, device_id=(lax.rem(dp + step, 32), z), device_id_type=MESH
+        )
+        return carry
+
+    lax.fori_loop(1, 32, greet, 0)
+    landing[dp] = mine_ref[...]
+    pl.semaphore_wait(barrier, 31)
+
+    def send(step, carry):
+        pltpu.make_async_remote_copy(
+            src_ref=mine_ref,
+            dst_ref=landing.at[dp],
+            send_sem=send_sem,
+            recv_sem=recv_sem,
+            device_id=(lax.rem(dp + step, 32), z),
+            device_id_type=MESH,
+        ).start()
+        return carry
+
+    lax.fori_loop(1, 32, send, 0)
+    all_of_them = landing.at[pl.ds(0, 31)]
+    pltpu.make_async_copy(all_of_them, all_of_them, recv_sem).wait()
+    pltpu.make_async_copy(all_of_them, all_of_them, send_sem).wait()
+
+    table = landing[:, 0, :]
+    lane = lax.broadcasted_iota(jnp.int32, (32, 128), 1)
+    line = lax.broadcasted_iota(jnp.int32, (32, 128), 0)
+
+    def column(k):
+        return jnp.sum(jnp.where(lane == k, table, 0), axis=1, keepdims=True)
+
+    parents = [column(0), column(1)]
+    rows = [
+        jnp.sum(jnp.where(lane == line, parent, 0), axis=0, keepdims=True) for parent in parents
+    ]
+    result = jnp.zeros((32, 128), jnp.int32)
+    low = jnp.full((1, 1), 9, jnp.int32)
+    high = jnp.full((1, 1), -1, jnp.int32)
+    for i in range(2):
+        before = jnp.zeros((32, 1), jnp.int32)
+        for row in rows:
+            same = jnp.right_shift(row, 2) == jnp.right_shift(parents[i], 2)
+            hit = same & (row < parents[i]) & (lane < 32)
+            before += jnp.sum(jnp.where(hit, 1, 0), axis=1, keepdims=True)
+        code = jnp.right_shift(parents[i], 2) * 2 + before
+        result = jnp.where(lane == i, code, result)
+        here = jnp.right_shift(parents[i], 2) == dp
+        slot = jnp.bitwise_and(parents[i], 3)
+        low = jnp.minimum(low, jnp.min(jnp.where(here, slot, 9), axis=0, keepdims=True))
+        high = jnp.maximum(high, jnp.max(jnp.where(here, slot, -1), axis=0, keepdims=True))
+        wanted = jnp.sum(
+            jnp.where(line[:, :1] == dp, parents[i], 0), axis=0, keepdims=True
+        )
+        found = (lane >= 2) & (lane < 6) & (line * 4 + lane - 2 == wanted)
+        extent = jnp.sum(
+            jnp.sum(jnp.where(found, table, 0), axis=0, keepdims=True), axis=1, keepdims=True
+        )
+        result = jnp.where(lane == 4 + i, extent, result)
+    result = jnp.where(lane == 2, low, result)
+    result = jnp.where(lane == 3, high, result)
+    out_ref[...] = result
+
+
+def make_table(kept_parent, stored_extent):
+    mine = jnp.concatenate([kept_parent, stored_extent])
+    mine = jnp.broadcast_to(jnp.pad(mine, (0, 122))[None], (8, 128))
+    vmem = pl.BlockSpec(memory_space=pltpu.VMEM)
+    return pl.pallas_call(
+        table_kernel,
+        out_shape=jax.ShapeDtypeStruct((32, 128), jnp.int32),
+        in_specs=[vmem],
+        out_specs=vmem,
+        scratch_shapes=[
+            pltpu.VMEM((32, 8, 128), jnp.int32),
+            pltpu.SemaphoreType.DMA,
+            pltpu.SemaphoreType.DMA,
+        ],
+        compiler_params=pltpu.CompilerParams(collective_id=2, has_side_effects=True),
+    )(mine)
+
+
+def route_kernel(
+    tab, k_ref, v_ref, kout, vout,
+    picked, gk, gv, s1, r1, s2, r2, fin, xin,
+    psend, precv, asend, arecv, fsend, frecv, s1s, s1r, s2s, s2r, xs, xr,
+):
+    dp, z, core, x, y = spots()
+    partner = (dp + 1 - 2 * core, z)
+    stores = (k_ref, v_ref)
+    outs = (kout, vout)
+    gathered = (gk, gv)
+    first_at = (x, y)
+    second_at = (y, x)
+
+    def at(kv, which, step):
+        along_x = (which == 0) == (kv == 0)
+        nx = lax.rem(x + step, 4) if along_x else x
+        ny = y if along_x else lax.rem(y + step, 4)
+        return ((ny * 4 + nx) * 2 + core, z)
+
+    def copy(src, dst, send, recv, target):
+        return pltpu.make_async_remote_copy(
+            src_ref=src, dst_ref=dst, send_sem=send, recv_sem=recv,
+            device_id=target, device_id_type=MESH,
+        )
+
+    def wait(ref, sem):
+        pltpu.make_async_copy(ref, ref, sem).wait()
+
+    barrier = pltpu.get_barrier_semaphore()
+    around = [partner] + [at(0, which, step) for which in range(2) for step in (1, 3)]
+    for other in around:
+        pl.semaphore_signal(barrier, inc=1, device_id=other, device_id_type=MESH)
+
+    mine_rows = pl.ds(pl.multiple_of(core * 256, 256), 256)
+    other_rows = pl.ds(pl.multiple_of((1 - core) * 256, 256), 256)
+    for kv in range(2):
+        for i in range(2):
+            picked[kv, i] = stores[kv][tab[0, 2 + i]]
+            gathered[kv][first_at[kv], core * 2 + i] = picked[kv, i, mine_rows, :]
+    pl.semaphore_wait(barrier, len(around))
+    swaps = []
+    for kv in range(2):
+        swaps.append(
+            copy(
+                picked.at[kv, pl.ds(0, 2), other_rows],
+                gathered[kv].at[first_at[kv], pl.ds(pl.multiple_of(core * 2, 2), 2)],
+                psend.at[kv], precv.at[kv], partner,
+            )
+        )
+        swaps[-1].start()
+
+    def pair(kv, place, half):
+        return gathered[kv].at[place, pl.ds(2 * half, 2)]
+
+    started = []
+    for kv in range(2):
+        mine = gathered[kv].at[first_at[kv], pl.ds(pl.multiple_of((1 - core) * 2, 2), 2)]
+        wait(mine, precv.at[kv])
+        for turn in range(2):
+            for way in range(2):
+                half = turn ^ way
+                block = pair(kv, first_at[kv], half)
+                started.append(
+                    copy(
+                        block, block, asend.at[kv, way, half], arecv.at[kv, way, half],
+                        at(kv, 0, 1 + 2 * way),
+                    )
+                )
+                started[-1].start()
+    for kv in range(2):
+        for way in range(2):
+            place = lax.rem(first_at[kv] + (3 if way == 0 else 1), 4)
+            block = pair(kv, place, way)
+            wait(block, arecv.at[kv, way, way])
+            started.append(
+                copy(block, block, fsend.at[kv, way], frecv.at[kv, way], at(kv, 0, 1 + 2 * way))
+            )
+            started[-1].start()
+    for kv in range(2):
+        for way in range(2):
+            place = lax.rem(first_at[kv] + (3 if way == 0 else 1), 4)
+            wait(pair(kv, place, 1 - way), arecv.at[kv, way, 1 - way])
+        for way in range(2):
+            wait(pair(kv, lax.rem(first_at[kv] + 2, 4), way), frecv.at[kv, way])
+
+    def candidate(kv, step, slot):
+        to = lax.rem(second_at[kv] + step, 4)
+        chip = to * 4 + x if kv == 0 else y * 4 + to
+        code = tab[chip * 2 + slot // 2, slot % 2]
+        rank = jnp.bitwise_and(code, 1)
+        source_core = jnp.bitwise_and(jnp.right_shift(code, 1), 1)
+        source_x = jnp.bitwise_and(jnp.right_shift(code, 2), 3)
+        source_y = jnp.right_shift(code, 4)
+        one, two = (source_x, source_y) if kv == 0 else (source_y, source_x)
+        return gathered[kv][one, source_core * 2 + rank], two
+
+    for kv in range(2):
+        for way in range(2):
+            for j in range(2):
+                s1[kv, way, j] = candidate(kv, 2, 2 * way + j)[0]
+            started.append(
+                copy(
+                    s1.at[kv, way], r1.at[kv, way], s1s.at[kv, way], s1r.at[kv, way],
+                    at(kv, 1, 1 + 2 * way),
+                )
+            )
+            started[-1].start()
+    for turn in range(2):
+        for kv in range(2):
+            for way in range(2):
+                half = 1 - way if turn == 0 else way
+                if turn == 1:
+                    wait(r1.at[kv, way], s1r.at[kv, way])
+                for j in range(2):
+                    slot = 2 * half + j
+                    value, two = candidate(kv, 1 + 2 * way, slot)
+                    if turn == 1:
+                        value = jnp.where(two == second_at[kv], value, r1[kv, way, j])
+                    s2[kv, way, slot] = value
+                started.append(
+                    copy(
+                        s2.at[kv, way, pl.ds(2 * half, 2)], r2.at[kv, way, pl.ds(2 * half, 2)],
+                        s2s.at[kv, way, half], s2r.at[kv, way, half], at(kv, 1, 1 + 2 * way),
+                    )
+                )
+                started[-1].start()
+    for kv in range(2):
+        for half in range(2):
+            for way in range(2):
+                wait(r2.at[kv, way, pl.ds(2 * half, 2)], s2r.at[kv, way, half])
+            for j in range(2):
+                slot = 2 * half + j
+                value, two = candidate(kv, 0, slot)
+                here = second_at[kv]
+                away = lax.rem(two - here + 4, 4)
+                first = (away == 3) | (away == 2) if half == 0 else away == 3
+                arrived = jnp.where(first, r2[kv, 0, slot], r2[kv, 1, slot])
+                fin[kv, slot] = jnp.where(away == 0, value, arrived)
+        theirs = fin.at[kv, pl.ds(pl.multiple_of((1 - core) * 2, 2), 2)]
+        started.append(copy(theirs, xin.at[kv], xs.at[kv], xr.at[kv], partner))
+        started[-1].start()
+        for i in range(2):
+            outs[kv][i, mine_rows, :] = fin[kv, core * 2 + i]
+    for kv in range(2):
+        wait(xin.at[kv], xr.at[kv])
+        for i in range(2):
+            outs[kv][i, other_rows, :] = xin[kv, i]
+    for each in swaps + started:
+        each.wait_send()
+
+
+def route(table, keys, values):
+    vmem = pl.BlockSpec(memory_space=pltpu.VMEM)
+    item = (256, 128)
+    bf16 = jnp.bfloat16
+    dma = pltpu.SemaphoreType.DMA
+    return pl.pallas_call(
+        route_kernel,
+        out_shape=[jax.ShapeDtypeStruct((2, 512, 128), bf16)] * 2,
+        in_specs=[pl.BlockSpec(memory_space=pltpu.SMEM), vmem, vmem],
+        out_specs=[vmem, vmem],
+        scratch_shapes=[
+            pltpu.VMEM((2, 2, 512, 128), bf16),
+            pltpu.VMEM((4, 4) + item, bf16),
+            pltpu.VMEM((4, 4) + item, bf16),
+            pltpu.VMEM((2, 2, 2) + item, bf16),
+            pltpu.VMEM((2, 2, 2) + item, bf16),
+            pltpu.VMEM((2, 2, 4) + item, bf16),
+            pltpu.VMEM((2, 2, 4) + item, bf16),
+            pltpu.VMEM((2, 4) + item, bf16),
+            pltpu.VMEM((2, 2) + item, bf16),
+            dma((2,)), dma((2,)),
+            dma((2, 2, 2)), dma((2, 2, 2)),
+            dma((2, 2)), dma((2, 2)),
+            dma((2, 2)), dma((2, 2)),
+            dma((2, 2, 2)), dma((2, 2, 2)),
+            dma((2,)), dma((2,)),
+        ],
+        compiler_params=pltpu.CompilerParams(
+            collective_id=3, has_side_effects=True, vmem_limit_bytes=40 * 1024 * 1024
+        ),
+    )(table, keys, values)
 
 
 def attend(
@@ -358,32 +636,9 @@
     final_projection_matrix,
     skip_stream,
 ):
-    tally_places = earlier_lookup_store.shape[0]
-    tally_lines = kept_parent.shape[0]
-    dp_count = lax.axis_size("dp")
-    device_rank_here = lax.axis_index("dp")
-    kept_parent_shared, extent_gathered_all = (
-        lax.all_gather(kept_parent, "dp", axis=0, tiled=True),
-        lax.all_gather(stored_extent, "dp", axis=0, tiled=True),
-    )
-    sender_device = kept_parent_shared // tally_places
-    device_place_shared = kept_parent_shared % tally_places
-    device_lines_here = lax.dynamic_slice_in_dim(
-        kept_parent_shared, device_rank_here * tally_lines, tally_lines
-    )
-    lengths = extent_gathered_all[device_lines_here]
-    from_here = (sender_device == device_rank_here).reshape(dp_count, tally_lines)
-    local_slot = device_place_shared.reshape(dp_count, tally_lines)
-    picked = jnp.sum(jnp.where(from_here, local_slot, 0), axis=1)
-    send_keys = earlier_lookup_store[picked]
-    send_values = earlier_content_store[picked]
-    recv_keys, recv_values = (
-        lax.all_to_all(send_keys, "dp", split_axis=0, concat_axis=0, tiled=True),
-        lax.all_to_all(send_values, "dp", split_axis=0, concat_axis=0, tiled=True),
-    )
-    my_sources = device_lines_here // tally_places
-    keys_in = recv_keys[my_sources]
-    values_in = recv_values[my_sources]
+    table = make_table(kept_parent, stored_extent)
+    keys_in, values_in = route(table, earlier_lookup_store, earlier_content_store)
+    lengths = table[0, 4:6]
     attended = attend(
         question_vectors,
         arriving_lookup_vectors,
@@ -392,7 +647,7 @@
         values_in,
         lengths,
     )
-    flat = attended.reshape(tally_lines * STRETCH, attended.shape[2])
+    flat = attended.reshape(attended.shape[0] * STRETCH, attended.shape[2])
     return project(flat, final_projection_matrix, skip_stream)
 
 

time: 253 us -> 156 us (0.62)
  the two profiles are of different devices: /device:TPU:23 before, /device:TPU:51 now
where the time goes in v2:
time: 156 us; the launch traced here: 155 us
  Pallas kernels  144 us (92%)
  local copies, waits for them, and re-layouts  5.36 us (3%)
  matrix products  3.27 us (2%)
  other arithmetic  2.44 us (2%)
    pallas_call x1, Pallas kernels, project(): pl.pallas_call(project_kernel, out_shape=jax.ShapeDtypeStruct(skip.shape,...  107 us
    pallas_call x1, Pallas kernels, route(): pl.pallas_call(route_kernel, out_shape=[jax.ShapeDtypeStruct((2, 512, 128...  27.6 us
    pallas_call x1, Pallas kernels, make_table(): pl.pallas_call(table_kernel, out_shape=jax.ShapeDtypeStruct((32, 128), jn...  9.87 us
    unnamed x16, local copies, waits for them, and re-layouts  3.71 us

profile of v2, /device:TPU:51, one launch (start us, length us, event | category | flops | bytes accessed | tf_op | source)
XLA Modules:
  0.0 155.3 jit_solution(12195089917788965648)
XLA Ops:
  0.0 0.0 copy-start
  0.0 0.8 pad_add_fusion
  0.8 0.6 broadcast_in_dim.50.mine_ref
  1.4 9.9 %shard_map.91.tab = s32[32,128]{1,0:T(8,128)} custom-call(s32[8,128]{1,0:T(8,128)} %broadcast_in_dim.50.mine_ref), custom_call_target="tpu_custom_call" | custom-call | tf_op jit(solution)/shard_map/pallas_call | solution.py:399
  11.3 0.7 slice_bitcast_fusion
  12.0 0.1 iota_compare_fusion.1
  12.1 0.2 iota_compare_fusion
  12.3 0.3 broadcast_select_fusion
  12.6 0.0 copy-start.1
  12.6 1.0 copy-done.1
  13.7 0.0 copy-start.2
  13.7 1.0 copy-done.2
  14.7 0.0 copy-start.3
  14.7 0.7 copy-done.3
  15.4 27.6 %shard_map.92 = (bf16[2,512,128]{2,1,0:T(8,128)(2,1)S(1)}, bf16[2,512,128]{2,1,0:T(8,128)(2,1)S(1)}) custom-call(s32[32,128]{1,0:T(8,128)S(1)} %copy-done.3, bf16[4,512,128]{2,1,0:T(8,128)(2,1)S(1)} %copy-done.1, bf16[4,512,128]{2,1,0:T(8,128)(2,1)S(1)} %copy-done.2), custom_call_target="tpu_custom_call" | custom-call | tf_op jit(solution)/shard_map/pallas_call | solution.py:569
  43.0 0.0 copy-done
  43.1 0.0 copy-start.6
  43.1 1.7 %fusion.1 = (f32[2,8,128]{2,1,0:T(8,128)S(1)}, f32[2,640,128,8]{2,1,3,0:T(8,128)S(1)}) fusion(pred[2,128,640]{1,2,0:T(8,128)(4,1)S(1)} %broadcast_select_fusion, bf16[2,128,128]{2,1,0:T(8,128)(2,1)} %param.10, bf16[2,512,128]{2,1,0:T(8,128)(2,1)S(1)} %get-tuple-element.8, bf16[2,128,1024]{2,1,0:T(8,128)(2,1)S(1)} %copy-done), kind=kOutput, calls=%fused_computation.4 | convolution fusion | flops 340129792 | bytes 6266880 | tf_op jit(solution)/shard_map/rcgqd,rkgd->rgqck/dot_general | solution.py:612
  44.8 1.1 fusion
  45.9 0.0 copy-done.6
  45.9 0.0 copy-start.4
  45.9 0.0 copy-start.5
  45.9 1.5 fusion.8
  47.5 0.3 copy.13
  47.8 0.1 copy.28
  47.9 0.0 copy-done.4
  47.9 0.0 copy-done.5
  47.9 106.5 %shard_map.93 = bf16[256,1024]{1,0:T(8,128)(2,1)S(1)} custom-call(bf16[256,1024]{1,0:T(8,128)(2,1)S(1)} %bitcast.57, bf16[1024,256]{1,0:T(8,128)(2,1)S(1)} %copy-done.4, bf16[256,1024]{1,0:T(8,128)(2,1)S(1)} %copy-done.5), custom_call_target="tpu_custom_call" | custom-call | flops 4294967296 | bytes 16777216 | tf_op jit(solution)/shard_map/pallas_call | solution.py:291
  154.5 0.8 copy.30
  (3 shorter events, 0.0 us)
Async XLA Ops:
  0.0 43.1 %copy-start = (bf16[2,128,1024]{2,1,0:T(8,128)(2,1)S(1)}, bf16[2,128,1024]{2,1,0:T(8,128)(2,1)}, u32[]{:S(2)}) copy-start(bf16[2,128,1024]{2,1,0:T(8,128)(2,1)} %param.9) | copy-start | bytes 1572868
  12.6 1.0 copy-start.1
  13.7 1.0 copy-start.2
  14.7 0.7 copy-start.3
  43.1 2.8 %copy-start.6 = (bf16[2,128,128]{2,1,0:T(8,128)(2,1)S(1)}, bf16[2,128,128]{2,1,0:T(8,128)(2,1)}, u32[]{:S(2)}) copy-start(bf16[2,128,128]{2,1,0:T(8,128)(2,1)} %param.11) | copy-start | bytes 196612
  45.9 2.0 %copy-start.4 = (bf16[1024,256]{1,0:T(8,128)(2,1)S(1)}, bf16[1024,256]{1,0:T(8,128)(2,1)}, u32[]{:S(2)}) copy-start(bf16[1024,256]{1,0:T(8,128)(2,1)} %w_ref.1) | copy-start | bytes 1572868
  45.9 2.0 %copy-start.5 = (bf16[256,1024]{1,0:T(8,128)(2,1)S(1)}, bf16[256,1024]{1,0:T(8,128)(2,1)}, u32[]{:S(2)}) copy-start(bf16[256,1024]{1,0:T(8,128)(2,1)} %skip_ref.1) | copy-start | bytes 1572868

commit v3 on v2

v3 whole, which is shorter than its diff:
```python
import math

import jax
import jax.numpy as jnp
from jax import lax
from jax.experimental import pallas as pl
from jax.experimental.pallas import tpu as pltpu
from jax.sharding import PartitionSpec as P

HEAD_DIM = 128
STRETCH = 128
CACHE = 512


MESH = pl.DeviceIdType.MESH
NEAR = [(1, 0), (3, 0), (0, 1), (0, 3)]
DIAGONAL = [(1, 1), (1, 3), (3, 1), (3, 3)]
FAR = [(2, 0), (0, 2), (2, 1), (2, 3), (1, 2), (3, 2), (2, 2)]


def spots():
    dp = lax.axis_index("dp")
    core = lax.rem(dp, 2)
    chip = dp // 2
    return dp, lax.axis_index("tensor"), core, lax.rem(chip, 4), chip // 4


def beside(axis, way):
    dp, z, core, x, y = spots()
    step = 1 + 2 * way
    nx = lax.rem(x + step, 4) if axis == 0 else x
    ny = y if axis == 0 else lax.rem(y + step, 4)
    return ((ny * 4 + nx) * 2 + core, z)


def wait_for(ref, sem):
    pltpu.make_async_copy(ref, ref, sem).wait()


def project_kernel(
    a_ref, own_ref, near_ref, diagonal_ref, far_ref, skip_ref, out_ref,
    a_buf, w_buf, s_buf, r_buf, t_buf, x_buf,
    rsem, ssem, asem, lsem, xsend, xrecv,
):
    dp, z, core, x, y = spots()
    partner = (dp + 1 - 2 * core, z)
    barrier = pltpu.get_barrier_semaphore()
    around = [partner, (dp, lax.rem(z + 1, 8)), (dp, lax.rem(z + 7, 8))]
    for other in around:
        pl.semaphore_signal(barrier, inc=1, device_id=other, device_id_type=MESH)

    sources = [((0, 0), own_ref)]
    for group, ref in ((NEAR, near_ref), (DIAGONAL, diagonal_ref), (FAR, far_ref)):
        sources += [(place, ref.at[k]) for k, place in enumerate(group)]
    loads = [
        pltpu.make_async_copy(ref, w_buf.at[dy * 4 + dx], lsem.at[dy * 4 + dx])
        for (dx, dy), ref in sources
    ]
    for load in loads:
        load.start()
    pl.semaphore_wait(barrier, len(around))
    exchange = pltpu.make_async_remote_copy(
        src_ref=a_ref, dst_ref=a_buf.at[core], send_sem=asem.at[0], recv_sem=asem.at[1],
        device_id=partner, device_id_type=MESH,
    )
    exchange.start()
    a_buf[core] = a_ref[...]
    for load in loads:
        load.wait()

    def product(d, h, k):
        goal = lax.rem(z + d, 8)
        dx = lax.rem(x - 2 * lax.rem(goal, 2) - k + 4, 4)
        dy = lax.rem(y - goal // 2 + 4, 4)
        return jnp.dot(a_buf[h], w_buf[dy * 4 + dx], preferred_element_type=jnp.float32)

    def step(s, carry):
        for turn in range(2):
            h = lax.rem(core + turn, 2)
            if turn == 1:

                @pl.when(s == 0)
                def _():
                    wait_for(a_buf.at[1 - core], asem.at[1])

            for k in range(2):
                for way in range(2):
                    d = 4 - s - h if way == 0 else 4 + s + 1 - h

                    @pl.when((d > 0) & (d < 8))
                    def _():
                        value = product(d, h, k)
                        place = ((s * 2 + k) * 2 + way) * 2 + h

                        @pl.when(s == 0)
                        def _():
                            s_buf[place] = value.astype(jnp.bfloat16)

                        @pl.when(s > 0)
                        def _():
                            before = jnp.maximum(s - 1, 0)
                            wait_for(r_buf.at[before, k, way, h], rsem.at[before, k, way, h])
                            s_buf[place] = (
                                value + r_buf[before, k, way, h].astype(jnp.float32)
                            ).astype(jnp.bfloat16)

                        pltpu.make_async_remote_copy(
                            src_ref=s_buf.at[place],
                            dst_ref=r_buf.at[s, k, way, h],
                            send_sem=ssem,
                            recv_sem=rsem.at[s, k, way, h],
                            device_id=(dp, lax.rem(z + 1 + 6 * way, 8)),
                            device_id_type=MESH,
                        ).start()
        return carry

    lax.fori_loop(0, 4, step, 0)

    def total(h, k):
        for way, last in ((0, 3 - h), (1, 2 + h)):
            wait_for(r_buf.at[last, k, way, h], rsem.at[last, k, way, h])
        return (
            t_buf[h, k]
            + r_buf[3 - h, k, 0, h].astype(jnp.float32)
            + r_buf[2 + h, k, 1, h].astype(jnp.float32)
        )

    for h in range(2):
        for k in range(2):
            t_buf[h, k] = product(0, h, k)
    sent = []
    for k in range(2):
        x_buf[0, k] = total(1 - core, k).astype(jnp.bfloat16)
        sent.append(
            pltpu.make_async_remote_copy(
                src_ref=x_buf.at[0, k], dst_ref=x_buf.at[1, k],
                send_sem=xsend.at[k], recv_sem=xrecv.at[k],
                device_id=partner, device_id_type=MESH,
            )
        )
        sent[-1].start()
    for k in range(2):
        columns = pl.ds(pl.multiple_of((2 * k + core) * 256, 256), 256)
        out_ref[:, columns] = (
            skip_ref[:, columns].astype(jnp.float32) + total(core, k)
        ).astype(jnp.bfloat16)
    for k in range(2):
        sent[k].wait_recv()
        columns = pl.ds(pl.multiple_of((2 * k + 1 - core) * 256, 256), 256)
        out_ref[:, columns] = (
            skip_ref[:, columns].astype(jnp.float32) + x_buf[1, k].astype(jnp.float32)
        ).astype(jnp.bfloat16)
    exchange.wait_send()
    for k in range(2):
        sent[k].wait_send()
    wait_for(s_buf.at[pl.ds(0, 28)], ssem)


def project(flat, own, near, diagonal, far, skip):
    vmem = pl.BlockSpec(memory_space=pltpu.VMEM)
    hbm = pl.BlockSpec(memory_space=pl.ANY)
    dma = pltpu.SemaphoreType.DMA
    return pl.pallas_call(
        project_kernel,
        out_shape=jax.ShapeDtypeStruct(skip.shape, skip.dtype),
        in_specs=[vmem, hbm, hbm, hbm, hbm, vmem],
        out_specs=vmem,
        scratch_shapes=[
            pltpu.VMEM((2, 256, 1024), jnp.bfloat16),
            pltpu.VMEM((16, 1024, 256), jnp.bfloat16),
            pltpu.VMEM((32, 256, 256), jnp.bfloat16),
            pltpu.VMEM((4, 2, 2, 2, 256, 256), jnp.bfloat16),
            pltpu.VMEM((2, 2, 256, 256), jnp.float32),
            pltpu.VMEM((2, 2, 256, 256), jnp.bfloat16),
            dma((4, 2, 2, 2)),
            dma,
            dma((2,)),
            dma((16,)),
            dma((2,)),
            dma((2,)),
        ],
        compiler_params=pltpu.CompilerParams(
            collective_id=1, has_side_effects=True, vmem_limit_bytes=60 * 1024 * 1024
        ),
        cost_estimate=pl.CostEstimate(
            flops=2 * 512 * 1024 * 4096, bytes_accessed=16 << 20, transcendentals=0
        ),
    )(flat, own, near, diagonal, far, skip)


def table_kernel(mine_ref, own_ref, out_ref, near_ref, landing, send_sem, recv_sem, wsend, wrecv):
    dp, z, _, _, _ = spots()
    barrier = pltpu.get_barrier_semaphore()

    def greet(step, carry):
        pl.semaphore_signal(
            barrier, inc=1, device_id=(lax.rem(dp + step, 32), z), device_id_type=MESH
        )
        return carry

    lax.fori_loop(1, 32, greet, 0)
    landing[dp] = mine_ref[...]
    pl.semaphore_wait(barrier, 31)

    def send(step, carry):
        pltpu.make_async_remote_copy(
            src_ref=mine_ref,
            dst_ref=landing.at[dp],
            send_sem=send_sem,
            recv_sem=recv_sem,
            device_id=(lax.rem(dp + step, 32), z),
            device_id_type=MESH,
        ).start()
        return carry

    lax.fori_loop(1, 32, send, 0)
    blocks = [
        pltpu.make_async_remote_copy(
            src_ref=own_ref, dst_ref=near_ref.at[axis * 2 + way],
            send_sem=wsend.at[axis, way], recv_sem=wrecv.at[axis, way],
            device_id=beside(axis, way), device_id_type=MESH,
        )
        for axis in range(2)
        for way in range(2)
    ]
    for block in blocks:
        block.start()
    all_of_them = landing.at[pl.ds(0, 31)]
    pltpu.make_async_copy(all_of_them, all_of_them, recv_sem).wait()
    pltpu.make_async_copy(all_of_them, all_of_them, send_sem).wait()

    table = landing[:, 0, :]
    lane = lax.broadcasted_iota(jnp.int32, (32, 128), 1)
    line = lax.broadcasted_iota(jnp.int32, (32, 128), 0)

    def column(k):
        return jnp.sum(jnp.where(lane == k, table, 0), axis=1, keepdims=True)

    parents = [column(0), column(1)]
    rows = [
        jnp.sum(jnp.where(lane == line, parent, 0), axis=0, keepdims=True) for parent in parents
    ]
    result = jnp.zeros((32, 128), jnp.int32)
    low = jnp.full((1, 1), 9, jnp.int32)
    high = jnp.full((1, 1), -1, jnp.int32)
    for i in range(2):
        before = jnp.zeros((32, 1), jnp.int32)
        for row in rows:
            same = jnp.right_shift(row, 2) == jnp.right_shift(parents[i], 2)
            hit = same & (row < parents[i]) & (lane < 32)
            before += jnp.sum(jnp.where(hit, 1, 0), axis=1, keepdims=True)
        code = jnp.right_shift(parents[i], 2) * 2 + before
        result = jnp.where(lane == i, code, result)
        here = jnp.right_shift(parents[i], 2) == dp
        slot = jnp.bitwise_and(parents[i], 3)
        low = jnp.minimum(low, jnp.min(jnp.where(here, slot, 9), axis=0, keepdims=True))
        high = jnp.maximum(high, jnp.max(jnp.where(here, slot, -1), axis=0, keepdims=True))
        wanted = jnp.sum(
            jnp.where(line[:, :1] == dp, parents[i], 0), axis=0, keepdims=True
        )
        found = (lane >= 2) & (lane < 6) & (line * 4 + lane - 2 == wanted)
        extent = jnp.sum(
            jnp.sum(jnp.where(found, table, 0), axis=0, keepdims=True), axis=1, keepdims=True
        )
        result = jnp.where(lane == 4 + i, extent, result)
    result = jnp.where(lane == 2, low, result)
    result = jnp.where(lane == 3, high, result)
    out_ref[...] = result
    for block in blocks:
        block.wait()


def make_table(kept_parent, stored_extent, own):
    mine = jnp.concatenate([kept_parent, stored_extent])
    mine = jnp.broadcast_to(jnp.pad(mine, (0, 122))[None], (8, 128))
    vmem = pl.BlockSpec(memory_space=pltpu.VMEM)
    return pl.pallas_call(
        table_kernel,
        out_shape=[
            jax.ShapeDtypeStruct((32, 128), jnp.int32),
            jax.ShapeDtypeStruct((4,) + own.shape, own.dtype),
        ],
        in_specs=[vmem, pl.BlockSpec(memory_space=pl.ANY)],
        out_specs=[vmem, pl.BlockSpec(memory_space=pl.ANY)],
        scratch_shapes=[
            pltpu.VMEM((32, 8, 128), jnp.int32),
            pltpu.SemaphoreType.DMA,
            pltpu.SemaphoreType.DMA,
            pltpu.SemaphoreType.DMA((2, 2)),
            pltpu.SemaphoreType.DMA((2, 2)),
        ],
        compiler_params=pltpu.CompilerParams(collective_id=2, has_side_effects=True, vmem_limit_bytes=60 * 1024 * 1024),
    )(mine, own)


PLACES = [[0], [1], [2], [3], [], [4], [5], [6]]


def route_kernel(
    tab, k_ref, v_ref, near_ref, kout, vout, diagonal_ref, far_ref,
    picked, gk, gv, s1, r1, s2, r2, fin, xin,
    psend, precv, asend, arecv, fsend, frecv, s1s, s1r, s2s, s2r, xs, xr, dgr, far_sem, wsend,
):
    dp, z, core, x, y = spots()
    partner = (dp + 1 - 2 * core, z)
    stores = (k_ref, v_ref)
    outs = (kout, vout)
    gathered = (gk, gv)
    first_at = (x, y)
    second_at = (y, x)

    def at(kv, which, step):
        along_x = (which == 0) == (kv == 0)
        nx = lax.rem(x + step, 4) if along_x else x
        ny = y if along_x else lax.rem(y + step, 4)
        return ((ny * 4 + nx) * 2 + core, z)

    def copy(src, dst, send, recv, target):
        return pltpu.make_async_remote_copy(
            src_ref=src, dst_ref=dst, send_sem=send, recv_sem=recv,
            device_id=target, device_id_type=MESH,
        )

    def wait(ref, sem):
        pltpu.make_async_copy(ref, ref, sem).wait()

    def push(source, to, sems, first, count, axis, way):
        rows = pl.ds(first * 256, count * 256)
        refs, sem = (diagonal_ref, dgr) if sems == 0 else (far_ref, far_sem)
        group = DIAGONAL if sems == 0 else FAR
        place = group.index(to)
        pltpu.make_async_remote_copy(
            src_ref=source.at[rows], dst_ref=refs.at[place, rows],
            send_sem=wsend.at[axis, way], recv_sem=sem.at[place, first // 2],
            device_id=beside(axis, way), device_id_type=MESH,
        ).start()

    def landed(place, half):
        k = FAR.index(place)
        wait(far_ref.at[k, pl.ds(half * 512, 512)], far_sem.at[k, half])

    def weights(part):
        if part == 0:
            for half in range(2):
                for way in range(2):
                    push(near_ref.at[way], (2, 0), 1, 2 * half + way, 1, 0, way)
                    push(near_ref.at[2 + way], (0, 2), 1, 2 * (1 - half) + way, 1, 1, way)
        if part in (1, 2):
            d = 2 * part - 1
            for way in range(2):
                push(near_ref.at[part - 1], (d, 1 + 2 * way), 0, 0, 2, 1, way)
                push(near_ref.at[1 + part], (1 + 2 * way, d), 0, 2, 2, 0, way)
        if part == 3:
            landed((2, 0), 0)
            landed((0, 2), 1)
            for way in range(2):
                push(far_ref.at[0], (2, 1 + 2 * way), 1, 0, 2, 1, way)
                push(far_ref.at[1], (1 + 2 * way, 2), 1, 2, 2, 0, way)
        if part == 4:
            for k in range(4):
                dx, dy = DIAGONAL[k]
                for half in range(2):
                    wait(diagonal_ref.at[k, pl.ds(half * 512, 512)], dgr.at[k, half])
                push(diagonal_ref.at[k], (dx, 2), 1, dy // 2, 1, 1, dy // 2)
                push(diagonal_ref.at[k], (2, dy), 1, 2 + dx // 2, 1, 0, dx // 2)
        if part == 5:
            for way in range(2):
                landed((2, 1 + 2 * way), 0)
                push(far_ref.at[FAR.index((2, 1 + 2 * way))], (2, 2), 1, way, 1, 1, way)
                landed((1 + 2 * way, 2), 1)
                push(far_ref.at[FAR.index((1 + 2 * way, 2))], (2, 2), 1, 2 + way, 1, 0, way)
        if part == 6:
            landed((2, 0), 1)
            landed((0, 2), 0)
            for way in range(2):
                landed((2, 1 + 2 * way), 1)
                landed((1 + 2 * way, 2), 0)
                landed((2, 2), way)
                for axis in range(2):
                    wait(far_ref.at[pl.ds(0, 4), pl.ds(0, 11 * 64)], wsend.at[axis, way])

    def at_point(point):
        for part in PLACES[point]:
            weights(part)

    barrier = pltpu.get_barrier_semaphore()
    around = [partner] + [at(0, which, step) for which in range(2) for step in (1, 3)]
    for other in around:
        pl.semaphore_signal(barrier, inc=1, device_id=other, device_id_type=MESH)

    mine_rows = pl.ds(pl.multiple_of(core * 256, 256), 256)
    other_rows = pl.ds(pl.multiple_of((1 - core) * 256, 256), 256)
    for kv in range(2):
        for i in range(2):
            picked[kv, i] = stores[kv][tab[0, 2 + i]]
            gathered[kv][first_at[kv], core * 2 + i] = picked[kv, i, mine_rows, :]
    pl.semaphore_wait(barrier, len(around))
    at_point(0)
    swaps = []
    for kv in range(2):
        swaps.append(
            copy(
                picked.at[kv, pl.ds(0, 2), other_rows],
                gathered[kv].at[first_at[kv], pl.ds(pl.multiple_of(core * 2, 2), 2)],
                psend.at[kv], precv.at[kv], partner,
            )
        )
        swaps[-1].start()

    def pair(kv, place, half):
        return gathered[kv].at[place, pl.ds(2 * half, 2)]

    started = []
    for kv in range(2):
        mine = gathered[kv].at[first_at[kv], pl.ds(pl.multiple_of((1 - core) * 2, 2), 2)]
        wait(mine, precv.at[kv])
        for turn in range(2):
            for way in range(2):
                half = turn ^ way
                block = pair(kv, first_at[kv], half)
                started.append(
                    copy(
                        block, block, asend.at[kv, way, half], arecv.at[kv, way, half],
                        at(kv, 0, 1 + 2 * way),
                    )
                )
                started[-1].start()
    at_point(1)
    for kv in range(2):
        for way in range(2):
            place = lax.rem(first_at[kv] + (3 if way == 0 else 1), 4)
            block = pair(kv, place, way)
            wait(block, arecv.at[kv, way, way])
            started.append(
                copy(block, block, fsend.at[kv, way], frecv.at[kv, way], at(kv, 0, 1 + 2 * way))
            )
            started[-1].start()
    at_point(2)
    for kv in range(2):
        for way in range(2):
            place = lax.rem(first_at[kv] + (3 if way == 0 else 1), 4)
            wait(pair(kv, place, 1 - way), arecv.at[kv, way, 1 - way])
        for way in range(2):
            wait(pair(kv, lax.rem(first_at[kv] + 2, 4), way), frecv.at[kv, way])

    def candidate(kv, step, slot):
        to = lax.rem(second_at[kv] + step, 4)
        chip = to * 4 + x if kv == 0 else y * 4 + to
        code = tab[chip * 2 + slot // 2, slot % 2]
        rank = jnp.bitwise_and(code, 1)
        source_core = jnp.bitwise_and(jnp.right_shift(code, 1), 1)
        source_x = jnp.bitwise_and(jnp.right_shift(code, 2), 3)
        source_y = jnp.right_shift(code, 4)
        one, two = (source_x, source_y) if kv == 0 else (source_y, source_x)
        return gathered[kv][one, source_core * 2 + rank], two

    for kv in range(2):
        for way in range(2):
            for j in range(2):
                s1[kv, way, j] = candidate(kv, 2, 2 * way + j)[0]
            started.append(
                copy(
                    s1.at[kv, way], r1.at[kv, way], s1s.at[kv, way], s1r.at[kv, way],
                    at(kv, 1, 1 + 2 * way),
                )
            )
            started[-1].start()
    at_point(3)
    for turn in range(2):
        if turn == 1:
            at_point(4)
        for kv in range(2):
            for way in range(2):
                half = 1 - way if turn == 0 else way
                if turn == 1:
                    wait(r1.at[kv, way], s1r.at[kv, way])
                for j in range(2):
                    slot = 2 * half + j
                    value, two = candidate(kv, 1 + 2 * way, slot)
                    if turn == 1:
                        value = jnp.where(two == second_at[kv], value, r1[kv, way, j])
                    s2[kv, way, slot] = value
                started.append(
                    copy(
                        s2.at[kv, way, pl.ds(2 * half, 2)], r2.at[kv, way, pl.ds(2 * half, 2)],
                        s2s.at[kv, way, half], s2r.at[kv, way, half], at(kv, 1, 1 + 2 * way),
                    )
                )
                started[-1].start()
    at_point(5)
    for kv in range(2):
        for half in range(2):
            for way in range(2):
                wait(r2.at[kv, way, pl.ds(2 * half, 2)], s2r.at[kv, way, half])
            for j in range(2):
                slot = 2 * half + j
                value, two = candidate(kv, 0, slot)
                here = second_at[kv]
                away = lax.rem(two - here + 4, 4)
                first = (away == 3) | (away == 2) if half == 0 else away == 3
                arrived = jnp.where(first, r2[kv, 0, slot], r2[kv, 1, slot])
                fin[kv, slot] = jnp.where(away == 0, value, arrived)
        theirs = fin.at[kv, pl.ds(pl.multiple_of((1 - core) * 2, 2), 2)]
        started.append(copy(theirs, xin.at[kv], xs.at[kv], xr.at[kv], partner))
        started[-1].start()
        for i in range(2):
            outs[kv][i, mine_rows, :] = fin[kv, core * 2 + i]
    at_point(6)
    for kv in range(2):
        wait(xin.at[kv], xr.at[kv])
        for i in range(2):
            outs[kv][i, other_rows, :] = xin[kv, i]
    at_point(7)
    for each in swaps + started:
        each.wait_send()


def route(table, keys, values, near):
    vmem = pl.BlockSpec(memory_space=pltpu.VMEM)
    item = (256, 128)
    hbm = pl.BlockSpec(memory_space=pl.ANY)
    bf16 = jnp.bfloat16
    dma = pltpu.SemaphoreType.DMA
    return pl.pallas_call(
        route_kernel,
        out_shape=[jax.ShapeDtypeStruct((2, 512, 128), bf16)] * 2
        + [jax.ShapeDtypeStruct((count,) + near.shape[1:], bf16) for count in (4, 7)],
        in_specs=[pl.BlockSpec(memory_space=pltpu.SMEM), vmem, vmem, hbm],
        out_specs=[vmem, vmem, hbm, hbm],
        scratch_shapes=[
            pltpu.VMEM((2, 2, 512, 128), bf16),
            pltpu.VMEM((4, 4) + item, bf16),
            pltpu.VMEM((4, 4) + item, bf16),
            pltpu.VMEM((2, 2, 2) + item, bf16),
            pltpu.VMEM((2, 2, 2) + item, bf16),
            pltpu.VMEM((2, 2, 4) + item, bf16),
            pltpu.VMEM((2, 2, 4) + item, bf16),
            pltpu.VMEM((2, 4) + item, bf16),
            pltpu.VMEM((2, 2) + item, bf16),
            dma((2,)), dma((2,)),
            dma((2, 2, 2)), dma((2, 2, 2)),
            dma((2, 2)), dma((2, 2)),
            dma((2, 2)), dma((2, 2)),
            dma((2, 2, 2)), dma((2, 2, 2)),
            dma((2,)), dma((2,)),
            dma((4, 2)), dma((7, 2)), dma((2, 2)),
        ],
        compiler_params=pltpu.CompilerParams(
            collective_id=3, has_side_effects=True, vmem_limit_bytes=60 * 1024 * 1024
        ),
    )(table, keys, values, near)


def attend(
    question_vectors, arriving_lookup_vectors, arriving_content_vectors, keys_in, values_in, lengths
):
    tally_lines = question_vectors.shape[0]
    groups = arriving_lookup_vectors.shape[2] // HEAD_DIM
    head_count = question_vectors.shape[2] // HEAD_DIM
    per_group = head_count // groups
    key_span = CACHE + STRETCH
    query_all = question_vectors.reshape(tally_lines, STRETCH, groups, per_group, HEAD_DIM)
    key_all = jnp.concatenate([keys_in, arriving_lookup_vectors], axis=1).reshape(
        tally_lines, key_span, groups, HEAD_DIM
    )
    value_all = jnp.concatenate([values_in, arriving_content_vectors], axis=1).reshape(
        tally_lines, key_span, groups, HEAD_DIM
    )
    scores = jnp.einsum(
        "rcgqd,rkgd->rgqck", query_all, key_all, preferred_element_type=jnp.float32
    ) / math.sqrt(HEAD_DIM)
    position = jnp.arange(key_span)
    query_pos = jnp.arange(STRETCH)
    in_cache = position[None, None, :] < lengths[:, None, None]
    in_stretch = position[None, :] - CACHE <= query_pos[:, None]
    allowed = jnp.where(position[None, None, :] < CACHE, in_cache, in_stretch[None])
    scores = jnp.where(allowed[:, None, None], scores, -jnp.inf)
    peak = jnp.max(scores, axis=-1, keepdims=True)
    raised = jnp.exp(scores - peak)
    probs = (raised / jnp.sum(raised, axis=-1, keepdims=True)).astype(jnp.bfloat16)
    mixed = jnp.einsum("rgqck,rkgd->rcgqd", probs, value_all, preferred_element_type=jnp.float32)
    return mixed.astype(jnp.bfloat16).reshape(tally_lines, STRETCH, head_count * HEAD_DIM)


def local(
    question_vectors,
    arriving_lookup_vectors,
    arriving_content_vectors,
    earlier_lookup_store,
    earlier_content_store,
    stored_extent,
    kept_parent,
    final_projection_matrix,
    skip_stream,
):
    table, near = make_table(kept_parent, stored_extent, final_projection_matrix)
    keys_in, values_in, diagonal, far = route(
        table, earlier_lookup_store, earlier_content_store, near
    )
    lengths = table[0, 4:6]
    attended = attend(
        question_vectors,
        arriving_lookup_vectors,
        arriving_content_vectors,
        keys_in,
        values_in,
        lengths,
    )
    flat = attended.reshape(attended.shape[0] * STRETCH, attended.shape[2])
    return project(flat, final_projection_matrix, near, diagonal, far, skip_stream)


def solution(mesh):
    return jax.shard_map(
        local,
        mesh=mesh,
        in_specs=(
            P("dp", None, "tensor"),
            P("dp", None, "tensor"),
            P("dp", None, "tensor"),
            P("dp", None, "tensor"),
            P("dp", None, "tensor"),
            P("dp"),
            P("dp"),
            P("tensor", "dp"),
            P("dp", "tensor"),
        ),
        out_specs=P("dp", "tensor"),
        check_vma=False,
    )
```

time: 156 us -> 140 us (0.90)
  the two profiles are of different devices: /device:TPU:51 before, /device:TPU:1 now
where the time goes in v3:
time: 140 us; the launch traced here: 139 us
  Pallas kernels  129 us (92%)
  local copies, waits for them, and re-layouts  4.44 us (3%)
  matrix products  3.43 us (2%)
  other arithmetic  2.44 us (2%)
    pallas_call x1, Pallas kernels, route(): pl.pallas_call(route_kernel, out_shape=[jax.ShapeDtypeStruct((2, 512, 128...  54.1 us
    pallas_call x1, Pallas kernels, project(): pl.pallas_call(project_kernel, out_shape=jax.ShapeDtypeStruct(skip.shape,...  51.7 us
    pallas_call x1, Pallas kernels, make_table(): pl.pallas_call(table_kernel, out_shape=[jax.ShapeDtypeStruct((32, 128), j...  23.1 us

profile of v3, /device:TPU:1, one launch (start us, length us, event | category | flops | bytes accessed | tf_op | source)
XLA Modules:
  0.0 139.3 jit_solution(6108987376627839875)
XLA Ops:
  0.0 0.0 copy-start
  0.0 0.8 pad_add_fusion
  0.8 0.6 broadcast_in_dim.50.mine_ref
  1.4 0.2 iota_compare_fusion
  1.6 23.1 %shard_map.91 = (s32[32,128]{1,0:T(8,128)}, bf16[4,1024,256]{2,1,0:T(8,128)(2,1)}) custom-call(s32[8,128]{1,0:T(8,128)} %broadcast_in_dim.50.mine_ref, bf16[1024,256]{1,0:T(8,128)(2,1)} %own_ref.3), custom_call_target="tpu_custom_call" | custom-call | tf_op jit(solution)/shard_map/pallas_call | solution.py:277
  24.7 0.8 slice_bitcast_fusion
  25.5 0.1 iota_compare_fusion.1
  25.5 0.3 broadcast_select_fusion
  25.9 54.1 %shard_map.92 = (bf16[2,512,128]{2,1,0:T(8,128)(2,1)}, bf16[2,512,128]{2,1,0:T(8,128)(2,1)}, bf16[4,1024,256]{2,1,0:T(8,128)(2,1)}, bf16[7,1024,256]{2,1,0:T(8,128)(2,1)}) custom-call(s32[32,128]{1,0:T(8,128)} %get-tuple-element.11.tab, bf16[4,512,128]{2,1,0:T(8,128)(2,1)} %k_ref.1, bf16[4,512,128]{2,1,0:T(8,128)(2,1)} %v_ref.1, ...), custom_call_target="tpu_custom_call" | custom-call | tf_op jit(solution)/shard_map/pallas_call | solution.py:524
  80.0 0.0 copy-done
  80.0 0.0 copy-start.1
  80.0 0.0 copy-start.2
  80.0 1.9 %fusion.1 = (f32[2,8,128]{2,1,0:T(8,128)S(1)}, f32[2,640,128,8]{2,1,3,0:T(8,128)S(1)}) fusion(pred[2,128,640]{1,2,0:T(8,128)(4,1)S(1)} %broadcast_select_fusion, bf16[2,128,128]{2,1,0:T(8,128)(2,1)} %param.10, bf16[2,512,128]{2,1,0:T(8,128)(2,1)} %get-tuple-element.14, bf16[2,128,1024]{2,1,0:T(8,128)(2,1)S(1)} %copy-done), kind=kOutput, calls=%fused_computation.4 | convolution fusion | flops 340129792 | bytes 6266880 | tf_op jit(solution)/shard_map/rcgqd,rkgd->rgqck/dot_general | solution.py:569
  81.9 1.1 fusion
  83.0 0.0 copy-done.1
  83.0 0.0 copy-done.2
  83.0 1.5 %fusion.8 = bf16[2,128,1,8,128]{1,4,3,0,2:T(8,128)(2,1)S(1)} fusion(f32[2,8,128]{2,1,0:T(8,128)S(1)} %fusion, f32[2,8,128]{2,1,0:T(8,128)S(1)} %get-tuple-element.17, f32[2,640,128,8]{2,1,3,0:T(8,128)S(1)} %get-tuple-element.18, pred[2,128,640]{1,2,0:T(8,128)(4,1)S(1)} %broadcast_select_fusion, bf16[2,128,128]{2,1,0:T(8,128)(2,1)S(1)} %copy-done.2, ...), kind=kOutput, calls=%fused_computation.9 | convolution fusion | flops 343015424 | bytes 6275072 | tf_op jit(solution)/shard_map/rgqck,rkgd->rcgqd/dot_general | solution.py:581
  84.6 0.3 copy.13
  84.9 0.9 copy.28
  85.8 51.7 %shard_map.93 = bf16[256,1024]{1,0:T(8,128)(2,1)} custom-call(bf16[256,1024]{1,0:T(8,128)(2,1)} %bitcast.58, bf16[1024,256]{1,0:T(8,128)(2,1)} %own_ref.3, bf16[4,1024,256]{2,1,0:T(8,128)(2,1)} %get-tuple-element.12.near_ref, bf16[4,1024,256]{2,1,0:T(8,128)(2,1)} %get-tuple-element.15.diagonal_ref, bf16[7,1024,256]{2,1,0:T(8,128)(2,1)} %get-tuple-element.16.far_ref, ...), custom_call_target="tpu_custom_call" | custom-call | flops 4294967296 | bytes 16777216 | tf_op jit(solution)/shard_map/pallas_call | solution.py:163
  137.4 1.9 %copy.30 = bf16[256,1024]{1,0:T(8,128)(2,1)} copy(bf16[256,1024]{1,0:T(8,128)(2,1)} %shard_map.93) | data formatting | bytes 1048576
  (3 shorter events, 0.0 us)
Async XLA Ops:
  0.0 80.0 %copy-start = (bf16[2,128,1024]{2,1,0:T(8,128)(2,1)S(1)}, bf16[2,128,1024]{2,1,0:T(8,128)(2,1)}, u32[]{:S(2)}) copy-start(bf16[2,128,1024]{2,1,0:T(8,128)(2,1)} %param.9) | copy-start | bytes 1572868
  80.0 3.0 %copy-start.1 = (bf16[2,512,128]{2,1,0:T(8,128)(2,1)S(1)}, bf16[2,512,128]{2,1,0:T(8,128)(2,1)}, u32[]{:S(2)}) copy-start(bf16[2,512,128]{2,1,0:T(8,128)(2,1)} %get-tuple-element.13) | copy-start | bytes 786436
  80.0 3.0 %copy-start.2 = (bf16[2,128,128]{2,1,0:T(8,128)(2,1)S(1)}, bf16[2,128,128]{2,1,0:T(8,128)(2,1)}, u32[]{:S(2)}) copy-start(bf16[2,128,128]{2,1,0:T(8,128)(2,1)} %param.11) | copy-start | bytes 196612

commit v4 on v0

v4 whole, which is shorter than its diff:
```python
import math

import jax
import jax.numpy as jnp
from jax import lax
from jax.experimental import pallas as pl
from jax.experimental.pallas import tpu as pltpu
from jax.sharding import PartitionSpec as P

HEAD_DIM = 128
STRETCH = 128
CACHE = 512
MESH = pl.DeviceIdType.MESH


def spots():
    dp = lax.axis_index("dp")
    core = lax.rem(dp, 2)
    chip = dp // 2
    return dp, lax.axis_index("tensor"), core, lax.rem(chip, 4), chip // 4


def beside(axis, way):
    dp, z, core, x, y = spots()
    step = 1 + 2 * way
    nx = lax.rem(x + step, 4) if axis == 0 else x
    ny = y if axis == 0 else lax.rem(y + step, 4)
    return ((ny * 4 + nx) * 2 + core, z)


def remote(src, dst, send, recv, target):
    return pltpu.make_async_remote_copy(
        src_ref=src, dst_ref=dst, send_sem=send, recv_sem=recv,
        device_id=target, device_id_type=MESH,
    )


def wait_for(ref, sem):
    pltpu.make_async_copy(ref, ref, sem).wait()


def row_table(table, dp):
    lane = lax.broadcasted_iota(jnp.int32, (32, 128), 1)
    line = lax.broadcasted_iota(jnp.int32, (32, 128), 0)

    def column(k):
        return jnp.sum(jnp.where(lane == k, table, 0), axis=1, keepdims=True)

    parents = [column(0), column(1)]
    rows = [
        jnp.sum(jnp.where(lane == line, parent, 0), axis=0, keepdims=True) for parent in parents
    ]
    result = jnp.zeros((32, 128), jnp.int32)
    low = jnp.full((1, 1), 9, jnp.int32)
    high = jnp.full((1, 1), -1, jnp.int32)
    for i in range(2):
        before = jnp.zeros((32, 1), jnp.int32)
        for row in rows:
            same = jnp.right_shift(row, 2) == jnp.right_shift(parents[i], 2)
            hit = same & (row < parents[i]) & (lane < 32)
            before += jnp.sum(jnp.where(hit, 1, 0), axis=1, keepdims=True)
        code = jnp.right_shift(parents[i], 2) * 2 + before
        result = jnp.where(lane == i, code, result)
        here = jnp.right_shift(parents[i], 2) == dp
        slot = jnp.bitwise_and(parents[i], 3)
        low = jnp.minimum(low, jnp.min(jnp.where(here, slot, 9), axis=0, keepdims=True))
        high = jnp.maximum(high, jnp.max(jnp.where(here, slot, -1), axis=0, keepdims=True))
        wanted = jnp.sum(jnp.where(line[:, :1] == dp, parents[i], 0), axis=0, keepdims=True)
        found = (lane >= 2) & (lane < 6) & (line * 4 + lane - 2 == wanted)
        extent = jnp.sum(
            jnp.sum(jnp.where(found, table, 0), axis=0, keepdims=True), axis=1, keepdims=True
        )
        result = jnp.where(lane == 4 + i, extent, result)
    result = jnp.where(lane == 2, jnp.minimum(low, 3), result)
    return jnp.where(lane == 3, jnp.maximum(high, 0), result)


NEAR = [(1, 0), (3, 0), (0, 1), (0, 3)]
DIAGONAL = [(1, 1), (1, 3), (3, 1), (3, 3)]
FAR = [(2, 0), (0, 2), (2, 1), (2, 3), (1, 2), (3, 2), (2, 2)]
PLACES = {"gather": [1], "forward": [2], "select": [0], "relay": [4], "own": [3], "row0": [5]}


def layer_kernel(
    mine_ref, q_ref, new_k_ref, new_v_ref, k_ref, v_ref, own_ref, skip_ref, out_ref,
    landing, tab_vmem, tab, w_buf,
    picked, gk, gv, s1, r1, s2, r2, fin, xin, all_k, all_v,
    a_buf, s_buf, r_buf, t_buf, x_buf,
    tsem, nsem, wsem, wsend,
    psend, precv, asend, arecv, fsend, frecv, s1s, s1r, s2s, s2r, xs, xr,
    rsem, ssem, esem, xsend, xrecv,
):
    dp, z, core, x, y = spots()
    partner = (dp + 1 - 2 * core, z)
    barrier = pltpu.get_barrier_semaphore()

    def greet(step, carry):
        pl.semaphore_signal(
            barrier, inc=1, device_id=(lax.rem(dp + step, 32), z), device_id_type=MESH
        )
        return carry

    lax.fori_loop(1, 32, greet, 0)
    for step in (1, 7):
        pl.semaphore_signal(
            barrier, inc=1, device_id=(dp, lax.rem(z + step, 8)), device_id_type=MESH
        )
    landing[dp] = mine_ref[...]
    w_buf[0] = own_ref[...]
    pl.semaphore_wait(barrier, 33)

    def share(step, carry):
        remote(
            mine_ref, landing.at[dp], tsem.at[0], tsem.at[1], (lax.rem(dp + step, 32), z)
        ).start()
        return carry

    lax.fori_loop(1, 32, share, 0)

    def slot_of(place):
        return place[1] * 4 + place[0]

    def sem_of(place, half):
        return wsem.at[(DIAGONAL + FAR).index(place), half]

    def push(source, to, first, count, axis, way):
        rows = pl.ds(first * 256, count * 256)
        remote(
            w_buf.at[slot_of(source), rows], w_buf.at[slot_of(to), rows],
            wsend.at[axis, way], sem_of(to, first // 2), beside(axis, way),
        ).start()

    def landed(place, half):
        wait_for(w_buf.at[slot_of(place), pl.ds(half * 512, 512)], sem_of(place, half))

    def weights(part):
        if part == 0:
            for half in range(2):
                for way in range(2):
                    push(NEAR[way], (2, 0), 2 * half + way, 1, 0, way)
                    push(NEAR[2 + way], (0, 2), 2 * (1 - half) + way, 1, 1, way)
        if part in (1, 2):
            d = 2 * part - 1
            for way in range(2):
                push(NEAR[part - 1], (d, 1 + 2 * way), 0, 2, 1, way)
                push(NEAR[part + 1], (1 + 2 * way, d), 2, 2, 0, way)
        if part == 3:
            landed((2, 0), 0)
            landed((0, 2), 1)
            for way in range(2):
                push((2, 0), (2, 1 + 2 * way), 0, 2, 1, way)
                push((0, 2), (1 + 2 * way, 2), 2, 2, 0, way)
        if part == 4:
            for dx, dy in DIAGONAL:
                for half in range(2):
                    landed((dx, dy), half)
                push((dx, dy), (dx, 2), dy // 2, 1, 1, dy // 2)
                push((dx, dy), (2, dy), 2 + dx // 2, 1, 0, dx // 2)
        if part == 5:
            for way in range(2):
                landed((2, 1 + 2 * way), 0)
                push((2, 1 + 2 * way), (2, 2), way, 1, 1, way)
                landed((1 + 2 * way, 2), 1)
                push((1 + 2 * way, 2), (2, 2), 2 + way, 1, 0, way)
        if part == 6:
            landed((2, 0), 1)
            landed((0, 2), 0)
            for way in range(2):
                landed((2, 1 + 2 * way), 1)
                landed((1 + 2 * way, 2), 0)
                landed((2, 2), way)

    def at_point(point):
        for part in PLACES.get(point, []):
            weights(part)

    for axis in range(2):
        for way in range(2):
            remote(
                w_buf.at[0], w_buf.at[slot_of(NEAR[axis * 2 + way])],
                wsend.at[axis, way], nsem.at[axis, way], beside(axis, way),
            ).start()

    all_of_them = landing.at[pl.ds(0, 31)]
    wait_for(all_of_them, tsem.at[1])
    tab_vmem[...] = row_table(landing[:, 0, :], dp)
    to_scalar = pltpu.make_async_copy(tab_vmem, tab, tsem.at[2])
    to_scalar.start()
    to_scalar.wait()

    stores = (k_ref, v_ref)
    gathered = (gk, gv)
    first_at = (x, y)
    second_at = (y, x)
    started = []

    def send(*args):
        started.append(remote(*args))
        started[-1].start()

    def at(kv, which, way):
        return beside(kv ^ which, way)

    mine_rows = pl.ds(pl.multiple_of(core * 256, 256), 256)
    other_rows = pl.ds(pl.multiple_of((1 - core) * 256, 256), 256)
    my_two = pl.ds(pl.multiple_of(core * 2, 2), 2)
    other_two = pl.ds(pl.multiple_of((1 - core) * 2, 2), 2)
    for kv in range(2):
        for i in range(2):
            picked[kv, i] = stores[kv][jnp.bitwise_and(tab[0, 2 + i], 3)]
            gathered[kv][first_at[kv], core * 2 + i] = picked[kv, i, mine_rows, :]
        send(
            picked.at[kv, pl.ds(0, 2), other_rows], gathered[kv].at[first_at[kv], my_two],
            psend.at[kv], precv.at[kv], partner,
        )

    def pair(kv, place, half):
        return gathered[kv].at[place, pl.ds(2 * half, 2)]

    for kv in range(2):
        wait_for(gathered[kv].at[first_at[kv], other_two], precv.at[kv])
        for turn in range(2):
            for way in range(2):
                half = turn ^ way
                block = pair(kv, first_at[kv], half)
                send(block, block, asend.at[kv, way, half], arecv.at[kv, way, half], at(kv, 0, way))
    for axis in range(2):
        for way in range(2):
            wait_for(w_buf.at[slot_of(NEAR[axis * 2 + way])], nsem.at[axis, way])
    at_point("gather")
    for kv in range(2):
        for way in range(2):
            block = pair(kv, lax.rem(first_at[kv] + (3 if way == 0 else 1), 4), way)
            wait_for(block, arecv.at[kv, way, way])
            send(block, block, fsend.at[kv, way], frecv.at[kv, way], at(kv, 0, way))
    at_point("forward")
    for kv in range(2):
        for way in range(2):
            place = lax.rem(first_at[kv] + (3 if way == 0 else 1), 4)
            wait_for(pair(kv, place, 1 - way), arecv.at[kv, way, 1 - way])
        for way in range(2):
            wait_for(pair(kv, lax.rem(first_at[kv] + 2, 4), way), frecv.at[kv, way])

    def candidate(kv, step, slot):
        to = lax.rem(second_at[kv] + step, 4)
        chip = to * 4 + x if kv == 0 else y * 4 + to
        code = tab[chip * 2 + slot // 2, slot % 2]
        rank = jnp.bitwise_and(code, 1)
        source_core = jnp.bitwise_and(jnp.right_shift(code, 1), 1)
        source_x = jnp.bitwise_and(jnp.right_shift(code, 2), 3)
        source_y = jnp.bitwise_and(jnp.right_shift(code, 4), 3)
        one, two = (source_x, source_y) if kv == 0 else (source_y, source_x)
        return gathered[kv][one, source_core * 2 + rank], two

    for kv in range(2):
        for way in range(2):
            for j in range(2):
                s1[kv, way, j] = candidate(kv, 2, 2 * way + j)[0]
            send(s1.at[kv, way], r1.at[kv, way], s1s.at[kv, way], s1r.at[kv, way], at(kv, 1, way))
    at_point("select")
    for turn in range(2):
        for kv in range(2):
            for way in range(2):
                half = 1 - way if turn == 0 else way
                if turn == 1:
                    wait_for(r1.at[kv, way], s1r.at[kv, way])
                for j in range(2):
                    slot = 2 * half + j
                    value, two = candidate(kv, 1 + 2 * way, slot)
                    if turn == 1:
                        value = jnp.where(two == second_at[kv], value, r1[kv, way, j])
                    s2[kv, way, slot] = value
                two_slots = pl.ds(2 * half, 2)
                send(
                    s2.at[kv, way, two_slots], r2.at[kv, way, two_slots],
                    s2s.at[kv, way, half], s2r.at[kv, way, half], at(kv, 1, way),
                )
        at_point("relay" if turn == 0 else "own")
    whole = (all_k, all_v)
    for kv in range(2):
        for half in range(2):
            for way in range(2):
                wait_for(r2.at[kv, way, pl.ds(2 * half, 2)], s2r.at[kv, way, half])
            for j in range(2):
                slot = 2 * half + j
                value, two = candidate(kv, 0, slot)
                away = lax.rem(two - second_at[kv] + 4, 4)
                first = (away == 3) | (away == 2) if half == 0 else away == 3
                arrived = jnp.where(first, r2[kv, 0, slot], r2[kv, 1, slot])
                fin[kv, slot] = jnp.where(away == 0, value, arrived)
        send(fin.at[kv, other_two], xin.at[kv], xs.at[kv], xr.at[kv], partner)
        for i in range(2):
            whole[kv][i, mine_rows, :] = fin[kv, core * 2 + i]
            whole[kv][i, pl.ds(CACHE, STRETCH), :] = (new_k_ref, new_v_ref)[kv][i]
    for kv in range(2):
        wait_for(xin.at[kv], xr.at[kv])
        for i in range(2):
            whole[kv][i, other_rows, :] = xin[kv, i]

    scale = 1.0 / math.sqrt(HEAD_DIM)
    span = CACHE + STRETCH
    exchange = []
    for i in range(2):
        position = lax.broadcasted_iota(jnp.int32, (2 * STRETCH, span), 1)
        token = lax.rem(lax.broadcasted_iota(jnp.int32, (2 * STRETCH, span), 0), STRETCH)
        bound = jnp.where(position < CACHE, tab[0, 4 + i], token + CACHE + 1)
        penalty = jnp.where(position < bound, 0.0, -1e30)
        tokens = pl.ds(i * STRETCH, STRETCH)

        def heads(c, carry):
            both = pl.ds(pl.multiple_of(c * 256, 256), 256)
            q = q_ref[i, :, both]
            q = jnp.concatenate([q[:, :HEAD_DIM], q[:, HEAD_DIM:]], axis=0)
            scores = lax.dot_general(
                q, all_k[i], (((1,), (1,)), ((), ())), preferred_element_type=jnp.float32
            )
            scores = scores * scale + penalty
            raised = jnp.exp(scores - jnp.max(scores, axis=1, keepdims=True))
            total = jnp.sum(raised, axis=1, keepdims=True)
            mixed = jnp.dot(
                raised.astype(jnp.bfloat16), all_v[i], preferred_element_type=jnp.float32
            )
            mixed = (mixed / total).astype(jnp.bfloat16)
            a_buf[core, tokens, both] = jnp.concatenate(
                [mixed[:STRETCH], mixed[STRETCH:]], axis=1
            )
            return carry

        lax.fori_loop(0, 4, heads, 0)
        exchange.append(
            remote(
                a_buf.at[core, tokens], a_buf.at[core, tokens],
                esem.at[0, i], esem.at[1, i], partner,
            )
        )
        exchange[-1].start()
        at_point("row%d" % i)
    weights(6)

    def product(d, h, k):
        goal = lax.rem(z + d, 8)
        dx = lax.rem(x - 2 * lax.rem(goal, 2) - k + 4, 4)
        dy = lax.rem(y - goal // 2 + 4, 4)
        return jnp.dot(a_buf[h], w_buf[dy * 4 + dx], preferred_element_type=jnp.float32)

    def step(s, carry):
        for turn in range(2):
            h = lax.rem(core + turn, 2)
            if turn == 1:

                @pl.when(s == 0)
                def _():
                    for i in range(2):
                        rows = pl.ds(i * STRETCH, STRETCH)
                        wait_for(a_buf.at[1 - core, rows], esem.at[1, i])

            for k in range(2):
                for way in range(2):
                    d = 4 - s - h if way == 0 else 4 + s + 1 - h

                    @pl.when((d > 0) & (d < 8))
                    def _():
                        value = product(d, h, k)
                        place = ((s * 2 + k) * 2 + way) * 2 + h

                        @pl.when(s == 0)
                        def _():
                            s_buf[place] = value.astype(jnp.bfloat16)

                        @pl.when(s > 0)
                        def _():
                            before = jnp.maximum(s - 1, 0)
                            wait_for(r_buf.at[before, k, way, h], rsem.at[before, k, way, h])
                            s_buf[place] = (
                                value + r_buf[before, k, way, h].astype(jnp.float32)
                            ).astype(jnp.bfloat16)

                        remote(
                            s_buf.at[place], r_buf.at[s, k, way, h],
                            ssem, rsem.at[s, k, way, h], (dp, lax.rem(z + 1 + 6 * way, 8)),
                        ).start()
        return carry

    lax.fori_loop(0, 4, step, 0)

    def total_of(h, k):
        for way, last in ((0, 3 - h), (1, 2 + h)):
            wait_for(r_buf.at[last, k, way, h], rsem.at[last, k, way, h])
        return (
            t_buf[h, k]
            + r_buf[3 - h, k, 0, h].astype(jnp.float32)
            + r_buf[2 + h, k, 1, h].astype(jnp.float32)
        )

    for h in range(2):
        for k in range(2):
            t_buf[h, k] = product(0, h, k)
    last = []
    for k in range(2):
        x_buf[0, k] = total_of(1 - core, k).astype(jnp.bfloat16)
        last.append(remote(x_buf.at[0, k], x_buf.at[1, k], xsend.at[k], xrecv.at[k], partner))
        last[-1].start()
    for k in range(2):
        columns = pl.ds(pl.multiple_of((2 * k + core) * 256, 256), 256)
        out_ref[:, columns] = (
            skip_ref[:, columns].astype(jnp.float32) + total_of(core, k)
        ).astype(jnp.bfloat16)
    for k in range(2):
        last[k].wait_recv()
        columns = pl.ds(pl.multiple_of((2 * k + 1 - core) * 256, 256), 256)
        out_ref[:, columns] = (
            skip_ref[:, columns].astype(jnp.float32) + x_buf[1, k].astype(jnp.float32)
        ).astype(jnp.bfloat16)
    for each in started + exchange + last:
        each.wait_send()
    wait_for(s_buf.at[pl.ds(0, 28)], ssem)
    wait_for(all_of_them, tsem.at[0])
    for axis in range(2):
        for way in range(2):
            wait_for(w_buf.at[pl.ds(0, 15), pl.ds(0, 256)], wsend.at[axis, way])


def local(
    question_vectors,
    arriving_lookup_vectors,
    arriving_content_vectors,
    earlier_lookup_store,
    earlier_content_store,
    stored_extent,
    kept_parent,
    final_projection_matrix,
    skip_stream,
):
    mine = jnp.concatenate([kept_parent, stored_extent])
    mine = jnp.broadcast_to(jnp.pad(mine, (0, 122))[None], (8, 128))
    vmem = pl.BlockSpec(memory_space=pltpu.VMEM)
    dma = pltpu.SemaphoreType.DMA
    bf16 = jnp.bfloat16
    item = (256, 128)
    return pl.pallas_call(
        layer_kernel,
        out_shape=jax.ShapeDtypeStruct(skip_stream.shape, skip_stream.dtype),
        in_specs=[vmem] * 8,
        out_specs=vmem,
        scratch_shapes=[
            pltpu.VMEM((32, 8, 128), jnp.int32),
            pltpu.VMEM((32, 128), jnp.int32),
            pltpu.SMEM((32, 128), jnp.int32),
            pltpu.VMEM((16, 1024, 256), bf16),
            pltpu.VMEM((2, 2, 512, 128), bf16),
            pltpu.VMEM((4, 4) + item, bf16),
            pltpu.VMEM((4, 4) + item, bf16),
            pltpu.VMEM((2, 2, 2) + item, bf16),
            pltpu.VMEM((2, 2, 2) + item, bf16),
            pltpu.VMEM((2, 2, 4) + item, bf16),
            pltpu.VMEM((2, 2, 4) + item, bf16),
            pltpu.VMEM((2, 4) + item, bf16),
            pltpu.VMEM((2, 2) + item, bf16),
            pltpu.VMEM((2, CACHE + STRETCH, HEAD_DIM), bf16),
            pltpu.VMEM((2, CACHE + STRETCH, HEAD_DIM), bf16),
            pltpu.VMEM((2, 256, 1024), bf16),
            pltpu.VMEM((32, 256, 256), bf16),
            pltpu.VMEM((4, 2, 2, 2, 256, 256), bf16),
            pltpu.VMEM((2, 2, 256, 256), jnp.float32),
            pltpu.VMEM((2, 2, 256, 256), bf16),
            dma((3,)), dma((2, 2)), dma((11, 2)), dma((2, 2)),
            dma((2,)), dma((2,)),
            dma((2, 2, 2)), dma((2, 2, 2)),
            dma((2, 2)), dma((2, 2)),
            dma((2, 2)), dma((2, 2)),
            dma((2, 2, 2)), dma((2, 2, 2)),
            dma((2,)), dma((2,)),
            dma((4, 2, 2, 2)), dma, dma((2, 2)), dma((2,)), dma((2,)),
        ],
        compiler_params=pltpu.CompilerParams(
            collective_id=1, has_side_effects=True, vmem_limit_bytes=56 * 1024 * 1024
        ),
        cost_estimate=pl.CostEstimate(
            flops=10 << 30, bytes_accessed=8 << 20, transcendentals=2 << 20
        ),
    )(
        mine,
        question_vectors,
        arriving_lookup_vectors,
        arriving_content_vectors,
        earlier_lookup_store,
        earlier_content_store,
        final_projection_matrix,
        skip_stream,
    )


def solution(mesh):
    return jax.shard_map(
        local,
        mesh=mesh,
        in_specs=(
            P("dp", None, "tensor"),
            P("dp", None, "tensor"),
            P("dp", None, "tensor"),
            P("dp", None, "tensor"),
            P("dp", None, "tensor"),
            P("dp"),
            P("dp"),
            P("tensor", "dp"),
            P("dp", "tensor"),
        ),
        out_specs=P("dp", "tensor"),
        check_vma=False,
    )
```

time: 256 us -> 124 us (0.48)
  waiting for transfers between devices: 171 us -> 0 us
  Pallas kernels: 0 us -> 120 us
  starting transfers between devices: 21.1 us -> 0 us
  between operations: 14.9 us -> 0.01 us
  blocking collectives: 14.4 us -> 0 us
  matrix products: 14.3 us -> 0 us
  local copies, waits for them, and re-layouts: 15.9 us -> 2.47 us
  other arithmetic: 3.91 us -> 0.75 us
    pallas_call x0 -> x1, Pallas kernels: none -> 120 us  [local(): pl.pallas_call(layer_kernel, out_shape=jax.ShapeDtypeStruct(skip_stream.s...]
    all_to_all x2 -> x0, waiting for transfers between devices: 114 us -> none  [the longest x1 60.9 us: local(): lax.all_to_all(send_keys, 'dp', split_axis=0, concat_axis=0, tiled=True)]
    reduce_scatter x1 -> x0, waiting for transfers between devices: 55.6 us -> none  [local(): lax.psum_scatter(terms.astype(jnp.bfloat16), 'tensor', scatter_dimension=...]
    all_to_all x2 -> x0, starting transfers between devices: 21 us -> none  [the longest x1 12.5 us: local(): lax.all_to_all(send_keys, 'dp', split_axis=0, concat_axis=0, tiled=True)]
    unnamed x1 -> x0, blocking collectives: 14.4 us -> none
    dot_general x3 -> x0, matrix products: 14.3 us -> none  [the longest x1 11.9 us: local(): jnp.dot(flat, lax.all_gather(final_projection_matrix, 'dp', axis=1, tiled...]
    gather x6 -> x0, local copies, waits for them, and re-layouts: 12.4 us -> none  [the longest x1 3.05 us: local(): send_keys = earlier_lookup_store[picked]]
  transfers between devices with their start and end apart: 4 -> 0, of which waited for: 3 -> 0; matrix products, arithmetic and copies ran while one was open for 8% -> 0% of each run, Pallas kernels for 0% -> 0%
where the time goes in v4:
time: 124 us
  Pallas kernels  120 us (97%)
  local copies, waits for them, and re-layouts  2.47 us (2%)
    pallas_call x1, Pallas kernels, local(): pl.pallas_call(layer_kernel, out_shape=jax.ShapeDtypeStruct(skip_stream.s...  120 us

profile of v4, /device:TPU:1, one launch (start us, length us, event | category | flops | bytes accessed | tf_op | source)
XLA Modules:
  0.0 123.7 jit_solution(13086745755924772875)
XLA Ops:
  0.0 0.7 pad_add_fusion
  0.8 0.6 broadcast_in_dim.2.mine_ref
  1.3 120.4 %shard_map.91 = bf16[256,1024]{1,0:T(8,128)(2,1)} custom-call(s32[8,128]{1,0:T(8,128)} %broadcast_in_dim.2.mine_ref, bf16[2,128,1024]{2,1,0:T(8,128)(2,1)} %q_ref.1, bf16[2,128,128]{2,1,0:T(8,128)(2,1)} %new_k_ref.1, bf16[2,128,128]{2,1,0:T(8,128)(2,1)} %new_v_ref.1, bf16[4,512,128]{2,1,0:T(8,128)(2,1)} %k_ref.1, bf16[4,512,128]{2,1,0:T(8,128)(2,1)} %v_ref.1, ...), custom_call_target="tpu_custom_call" | custom-call | flops 10737418240 | bytes 8388608 | tf_op jit(solution)/shard_map/pallas_call | solution.py:440
  121.8 1.9 %copy.11 = bf16[256,1024]{1,0:T(8,128)(2,1)} copy(bf16[256,1024]{1,0:T(8,128)(2,1)} %shard_map.91) | data formatting | bytes 1048576
  (1 shorter events, 0.0 us)

commit v5 on v4

--- a/solution.py
+++ b/solution.py
@@ -78,7 +78,17 @@
 NEAR = [(1, 0), (3, 0), (0, 1), (0, 3)]
 DIAGONAL = [(1, 1), (1, 3), (3, 1), (3, 3)]
 FAR = [(2, 0), (0, 2), (2, 1), (2, 3), (1, 2), (3, 2), (2, 2)]
-PLACES = {"gather": [1], "forward": [2], "select": [0], "relay": [4], "own": [3], "row0": [5]}
+PLACES = {
+    "start": ["own"],
+    "gather": [],
+    "forward": ["side 0"],
+    "select": ["own b", "far b"],
+    "relay": [],
+    "own": ["side 1"],
+    "swap": ["odd"],
+    "row0": ["own a", "even"],
+    "row1": [],
+}
 
 
 def layer_kernel(
@@ -86,7 +96,7 @@
     landing, tab_vmem, tab, w_buf,
     picked, gk, gv, s1, r1, s2, r2, fin, xin, all_k, all_v,
     a_buf, s_buf, r_buf, t_buf, x_buf,
-    tsem, nsem, wsem, wsend,
+    tsem, wsem, wsend,
     psend, precv, asend, arecv, fsend, frecv, s1s, s1r, s2s, s2r, xs, xr,
     rsem, ssem, esem, xsend, xrecv,
 ):
@@ -121,7 +131,7 @@
         return place[1] * 4 + place[0]
 
     def sem_of(place, half):
-        return wsem.at[(DIAGONAL + FAR).index(place), half]
+        return wsem.at[(NEAR + DIAGONAL + FAR).index(place), half]
 
     def push(source, to, first, count, axis, way):
         rows = pl.ds(first * 256, count * 256)
@@ -134,53 +144,70 @@
         wait_for(w_buf.at[slot_of(place), pl.ds(half * 512, 512)], sem_of(place, half))
 
     def weights(part):
-        if part == 0:
-            for half in range(2):
-                for way in range(2):
-                    push(NEAR[way], (2, 0), 2 * half + way, 1, 0, way)
-                    push(NEAR[2 + way], (0, 2), 2 * (1 - half) + way, 1, 1, way)
-        if part in (1, 2):
-            d = 2 * part - 1
-            for way in range(2):
-                push(NEAR[part - 1], (d, 1 + 2 * way), 0, 2, 1, way)
-                push(NEAR[part + 1], (1 + 2 * way, d), 2, 2, 0, way)
-        if part == 3:
+        if part == "own":
+            for way in range(2):
+                push((0, 0), (1 + 2 * way, 0), 0, 2, 0, way)
+                push((0, 0), (0, 1 + 2 * way), 2, 2, 1, way)
+        if part == "own b":
+            for way in range(2):
+                push((0, 0), (1 + 2 * way, 0), 2, 2, 0, way)
+        if part in ("side 0", "side 1"):
+            d = 1 if part == "side 0" else 3
+            landed((d, 0), 0)
+            landed((0, d), 1)
+            for way in range(2):
+                push((d, 0), (d, 1 + 2 * way), 0, 2, 1, way)
+                push((0, d), (1 + 2 * way, d), 2, 2, 0, way)
+            if d == 3:
+                push((0, 3), (0, 2), 3, 1, 1, 1)
+        if part == "far b":
+            push((0, 1), (0, 2), 2, 1, 1, 0)
+        if part == "odd":
+            landed((0, 2), 1)
+            for way in range(2):
+                push((0, 2), (1 + 2 * way, 2), 2, 2, 0, way)
+            for dx, dy in DIAGONAL:
+                landed((dx, dy), 0)
+                push((dx, dy), (dx, 2), dy // 2, 1, 1, dy // 2)
+        if part == "own a":
+            for way in range(2):
+                push((0, 0), (0, 1 + 2 * way), 0, 2, 1, way)
+        if part == "even":
+            for way in range(2):
+                landed((1 + 2 * way, 0), 1)
+                for half in range(2):
+                    push((1 + 2 * way, 0), (2, 0), 2 * half + way, 1, 0, way)
+        if part == "odd done":
+            for dx, dy in DIAGONAL:
+                landed((dx, dy), 1)
+                push((dx, dy), (2, dy), 2 + dx // 2, 1, 0, dx // 2)
+            for dx in (1, 3):
+                landed((dx, 2), 1)
+                push((dx, 2), (2, 2), 2 + dx // 2, 1, 0, dx // 2)
+                landed((dx, 2), 0)
+        if part == "even 1":
             landed((2, 0), 0)
-            landed((0, 2), 1)
             for way in range(2):
                 push((2, 0), (2, 1 + 2 * way), 0, 2, 1, way)
-                push((0, 2), (1 + 2 * way, 2), 2, 2, 0, way)
-        if part == 4:
-            for dx, dy in DIAGONAL:
-                for half in range(2):
-                    landed((dx, dy), half)
-                push((dx, dy), (dx, 2), dy // 2, 1, 1, dy // 2)
-                push((dx, dy), (2, dy), 2 + dx // 2, 1, 0, dx // 2)
-        if part == 5:
+            for way in range(2):
+                landed((0, 1 + 2 * way), 0)
+                push((0, 1 + 2 * way), (0, 2), way, 1, 1, way)
+        if part == "even 2":
             for way in range(2):
                 landed((2, 1 + 2 * way), 0)
                 push((2, 1 + 2 * way), (2, 2), way, 1, 1, way)
-                landed((1 + 2 * way, 2), 1)
-                push((1 + 2 * way, 2), (2, 2), 2 + way, 1, 0, way)
-        if part == 6:
+        if part == "even done":
             landed((2, 0), 1)
             landed((0, 2), 0)
             for way in range(2):
                 landed((2, 1 + 2 * way), 1)
-                landed((1 + 2 * way, 2), 0)
                 landed((2, 2), way)
 
     def at_point(point):
-        for part in PLACES.get(point, []):
+        for part in PLACES[point]:
             weights(part)
 
-    for axis in range(2):
-        for way in range(2):
-            remote(
-                w_buf.at[0], w_buf.at[slot_of(NEAR[axis * 2 + way])],
-                wsend.at[axis, way], nsem.at[axis, way], beside(axis, way),
-            ).start()
-
+    at_point("start")
     all_of_them = landing.at[pl.ds(0, 31)]
     wait_for(all_of_them, tsem.at[1])
     tab_vmem[...] = row_table(landing[:, 0, :], dp)
@@ -224,9 +251,6 @@
                 half = turn ^ way
                 block = pair(kv, first_at[kv], half)
                 send(block, block, asend.at[kv, way, half], arecv.at[kv, way, half], at(kv, 0, way))
-    for axis in range(2):
-        for way in range(2):
-            wait_for(w_buf.at[slot_of(NEAR[axis * 2 + way])], nsem.at[axis, way])
     at_point("gather")
     for kv in range(2):
         for way in range(2):
@@ -292,6 +316,7 @@
         for i in range(2):
             whole[kv][i, mine_rows, :] = fin[kv, core * 2 + i]
             whole[kv][i, pl.ds(CACHE, STRETCH), :] = (new_k_ref, new_v_ref)[kv][i]
+    at_point("swap")
     for kv in range(2):
         wait_for(xin.at[kv], xr.at[kv])
         for i in range(2):
@@ -335,7 +360,7 @@
         )
         exchange[-1].start()
         at_point("row%d" % i)
-    weights(6)
+    weights("odd done")
 
     def product(d, h, k):
         goal = lax.rem(z + d, 8)
@@ -343,75 +368,100 @@
         dy = lax.rem(y - goal // 2 + 4, 4)
         return jnp.dot(a_buf[h], w_buf[dy * 4 + dx], preferred_element_type=jnp.float32)
 
-    def step(s, carry):
+    def columns_of(round_):
+        return lax.rem(x + 1 + round_, 2)
+
+    def final(round_):
+        k = columns_of(round_)
+
+        def total_of(h):
+            value = product(0, h, k)
+            for way, end in ((0, 3 - h), (1, 2 + h)):
+                for u in range(2):
+                    rows = pl.ds(u * 128, 128)
+                    wait_for(
+                        r_buf.at[end, round_, way, h, rows], rsem.at[end, round_, way, h, u]
+                    )
+                value += r_buf[end, round_, way, h].astype(jnp.float32)
+            return value
+
+        x_buf[0, round_] = total_of(1 - core).astype(jnp.bfloat16)
+        remote(
+            x_buf.at[0, round_], x_buf.at[1, round_], xsend.at[round_], xrecv.at[round_], partner
+        ).start()
+        columns = pl.ds(pl.multiple_of((2 * k + core) * 256, 256), 256)
+        out_ref[:, columns] = (
+            skip_ref[:, columns].astype(jnp.float32) + total_of(core)
+        ).astype(jnp.bfloat16)
+
+    def step(i, carry):
+        round_ = i // 4
+        s = lax.rem(i, 4)
+        k = columns_of(round_)
+        for when, part in ((1, "even 1"), (3, "even 2"), (4, "even done")):
+
+            @pl.when(i == when)
+            def _():
+                weights(part)
+
+        @pl.when(i == 6)
+        def _():
+            final(0)
+
         for turn in range(2):
             h = lax.rem(core + turn, 2)
             if turn == 1:
 
-                @pl.when(s == 0)
+                @pl.when(i == 0)
                 def _():
-                    for i in range(2):
-                        rows = pl.ds(i * STRETCH, STRETCH)
-                        wait_for(a_buf.at[1 - core, rows], esem.at[1, i])
-
-            for k in range(2):
-                for way in range(2):
-                    d = 4 - s - h if way == 0 else 4 + s + 1 - h
-
-                    @pl.when((d > 0) & (d < 8))
-                    def _():
-                        value = product(d, h, k)
-                        place = ((s * 2 + k) * 2 + way) * 2 + h
+                    for row in range(2):
+                        rows = pl.ds(row * STRETCH, STRETCH)
+                        wait_for(a_buf.at[1 - core, rows], esem.at[1, row])
+
+            for way in range(2):
+                d = 4 - s - h if way == 0 else 4 + s + 1 - h
+
+                @pl.when((d > 0) & (d < 8))
+                def _():
+                    place = ((s * 2 + round_) * 2 + way) * 2 + h
+                    t_buf[...] = product(d, h, k)
+                    for u in range(2):
+                        rows = pl.ds(u * 128, 128)
 
                         @pl.when(s == 0)
                         def _():
-                            s_buf[place] = value.astype(jnp.bfloat16)
+                            s_buf[place, rows, :] = t_buf[rows, :].astype(jnp.bfloat16)
 
                         @pl.when(s > 0)
                         def _():
                             before = jnp.maximum(s - 1, 0)
-                            wait_for(r_buf.at[before, k, way, h], rsem.at[before, k, way, h])
-                            s_buf[place] = (
-                                value + r_buf[before, k, way, h].astype(jnp.float32)
+                            wait_for(
+                                r_buf.at[before, round_, way, h, rows],
+                                rsem.at[before, round_, way, h, u],
+                            )
+                            s_buf[place, rows, :] = (
+                                t_buf[rows, :]
+                                + r_buf[before, round_, way, h, rows, :].astype(jnp.float32)
                             ).astype(jnp.bfloat16)
 
                         remote(
-                            s_buf.at[place], r_buf.at[s, k, way, h],
-                            ssem, rsem.at[s, k, way, h], (dp, lax.rem(z + 1 + 6 * way, 8)),
+                            s_buf.at[place, rows], r_buf.at[s, round_, way, h, rows],
+                            ssem, rsem.at[s, round_, way, h, u],
+                            (dp, lax.rem(z + 1 + 6 * way, 8)),
                         ).start()
         return carry
 
-    lax.fori_loop(0, 4, step, 0)
-
-    def total_of(h, k):
-        for way, last in ((0, 3 - h), (1, 2 + h)):
-            wait_for(r_buf.at[last, k, way, h], rsem.at[last, k, way, h])
-        return (
-            t_buf[h, k]
-            + r_buf[3 - h, k, 0, h].astype(jnp.float32)
-            + r_buf[2 + h, k, 1, h].astype(jnp.float32)
-        )
-
-    for h in range(2):
-        for k in range(2):
-            t_buf[h, k] = product(0, h, k)
-    last = []
-    for k in range(2):
-        x_buf[0, k] = total_of(1 - core, k).astype(jnp.bfloat16)
-        last.append(remote(x_buf.at[0, k], x_buf.at[1, k], xsend.at[k], xrecv.at[k], partner))
-        last[-1].start()
-    for k in range(2):
-        columns = pl.ds(pl.multiple_of((2 * k + core) * 256, 256), 256)
-        out_ref[:, columns] = (
-            skip_ref[:, columns].astype(jnp.float32) + total_of(core, k)
-        ).astype(jnp.bfloat16)
-    for k in range(2):
-        last[k].wait_recv()
+    lax.fori_loop(0, 8, step, 0)
+    final(1)
+    for round_ in range(2):
+        k = columns_of(round_)
+        wait_for(x_buf.at[1, round_], xrecv.at[round_])
         columns = pl.ds(pl.multiple_of((2 * k + 1 - core) * 256, 256), 256)
         out_ref[:, columns] = (
-            skip_ref[:, columns].astype(jnp.float32) + x_buf[1, k].astype(jnp.float32)
+            skip_ref[:, columns].astype(jnp.float32) + x_buf[1, round_].astype(jnp.float32)
         ).astype(jnp.bfloat16)
-    for each in started + exchange + last:
+        wait_for(x_buf.at[0, round_], xsend.at[round_])
+    for each in started + exchange:
         each.wait_send()
     wait_for(s_buf.at[pl.ds(0, 28)], ssem)
     wait_for(all_of_them, tsem.at[0])
@@ -461,16 +511,16 @@
             pltpu.VMEM((2, 256, 1024), bf16),
             pltpu.VMEM((32, 256, 256), bf16),
             pltpu.VMEM((4, 2, 2, 2, 256, 256), bf16),
-            pltpu.VMEM((2, 2, 256, 256), jnp.float32),
+            pltpu.VMEM((256, 256), jnp.float32),
             pltpu.VMEM((2, 2, 256, 256), bf16),
-            dma((3,)), dma((2, 2)), dma((11, 2)), dma((2, 2)),
+            dma((3,)), dma((15, 2)), dma((2, 2)),
             dma((2,)), dma((2,)),
             dma((2, 2, 2)), dma((2, 2, 2)),
             dma((2, 2)), dma((2, 2)),
             dma((2, 2)), dma((2, 2)),
             dma((2, 2, 2)), dma((2, 2, 2)),
             dma((2,)), dma((2,)),
-            dma((4, 2, 2, 2)), dma, dma((2, 2)), dma((2,)), dma((2,)),
+            dma((4, 2, 2, 2, 2)), dma, dma((2, 2)), dma((2,)), dma((2,)),
         ],
         compiler_params=pltpu.CompilerParams(
             collective_id=1, has_side_effects=True, vmem_limit_bytes=56 * 1024 * 1024

time: 124 us -> 111 us (0.90)
  Pallas kernels: 120 us -> 108 us
    pallas_call x1, Pallas kernels: 120 us -> 108 us  [local(): pl.pallas_call(layer_kernel, out_shape=jax.ShapeDtypeStruct(skip_stream.s...]
where the time goes in v5:
time: 111 us
  Pallas kernels  108 us (97%)
  local copies, waits for them, and re-layouts  2.47 us (2%)
    pallas_call x1, Pallas kernels, local(): pl.pallas_call(layer_kernel, out_shape=jax.ShapeDtypeStruct(skip_stream.s...  108 us

profile of v5, /device:TPU:1, one launch (start us, length us, event | category | flops | bytes accessed | tf_op | source)
XLA Modules:
  0.0 110.8 jit_solution(15016991688411903823)
XLA Ops:
  0.0 0.7 pad_add_fusion
  0.8 0.6 broadcast_in_dim.2.mine_ref
  1.3 107.6 %shard_map.91 = bf16[256,1024]{1,0:T(8,128)(2,1)} custom-call(s32[8,128]{1,0:T(8,128)} %broadcast_in_dim.2.mine_ref, bf16[2,128,1024]{2,1,0:T(8,128)(2,1)} %q_ref.1, bf16[2,128,128]{2,1,0:T(8,128)(2,1)} %new_k_ref.1, bf16[2,128,128]{2,1,0:T(8,128)(2,1)} %new_v_ref.1, bf16[4,512,128]{2,1,0:T(8,128)(2,1)} %k_ref.1, bf16[4,512,128]{2,1,0:T(8,128)(2,1)} %v_ref.1, ...), custom_call_target="tpu_custom_call" | custom-call | flops 10737418240 | bytes 8388608 | tf_op jit(solution)/shard_map/pallas_call | solution.py:490
  108.9 1.9 %copy.11 = bf16[256,1024]{1,0:T(8,128)(2,1)} copy(bf16[256,1024]{1,0:T(8,128)(2,1)} %shard_map.91) | data formatting | bytes 1048576
  (1 shorter events, 0.0 us)

commit v6 on v5

--- a/solution.py
+++ b/solution.py
@@ -78,142 +78,159 @@
 NEAR = [(1, 0), (3, 0), (0, 1), (0, 3)]
 DIAGONAL = [(1, 1), (1, 3), (3, 1), (3, 3)]
 FAR = [(2, 0), (0, 2), (2, 1), (2, 3), (1, 2), (3, 2), (2, 2)]
-PLACES = {
-    "start": ["own"],
-    "gather": [],
-    "forward": ["side 0"],
-    "select": ["own b", "far b"],
-    "relay": [],
-    "own": ["side 1"],
-    "swap": ["odd"],
-    "row0": ["own a", "even"],
-    "row1": [],
+PLACES = {'start': [('own a', 0), ('own b', 0)], 'gather': [], 'forward': [('side', 0)], 'select': [('far', 0)], 'relay': [], 'own': [('diagonal', 0), ('far side', 0), ('own a', 1)], 'swap': [('corner', 0)], 'row0': [('own b', 1)], 'row1': [('done', 0)]}
+SERVICES = {
+    (0, 1): ("side", 1),
+    (1, 0): ("far", 1),
+    (2, 0): ("diagonal", 1),
+    (2, 1): ("far side", 1),
+    (3, 1): ("corner", 1),
+    (4, 0): ("done", 1),
 }
 
 
 def layer_kernel(
-    mine_ref, q_ref, new_k_ref, new_v_ref, k_ref, v_ref, own_ref, skip_ref, out_ref,
-    landing, tab_vmem, tab, w_buf,
+    parent_ref, extent_ref, q_hbm, new_k_hbm, new_v_hbm, k_hbm, v_hbm, own_ref, skip_hbm, out_ref,
+    landing, tab_vmem, tab, w_buf, q_ref, new_k_ref, new_v_ref, k_ref, v_ref, skip_ref,
     picked, gk, gv, s1, r1, s2, r2, fin, xin, all_k, all_v,
     a_buf, s_buf, r_buf, t_buf, x_buf,
-    tsem, wsem, wsend,
+    tsem, lsem, wsem, wsend,
     psend, precv, asend, arecv, fsend, frecv, s1s, s1r, s2s, s2r, xs, xr,
     rsem, ssem, esem, xsend, xrecv,
 ):
     dp, z, core, x, y = spots()
+    chip = dp // 2
     partner = (dp + 1 - 2 * core, z)
     barrier = pltpu.get_barrier_semaphore()
 
-    def greet(step, carry):
-        pl.semaphore_signal(
-            barrier, inc=1, device_id=(lax.rem(dp + step, 32), z), device_id_type=MESH
-        )
-        return carry
-
-    lax.fori_loop(1, 32, greet, 0)
-    for step in (1, 7):
-        pl.semaphore_signal(
-            barrier, inc=1, device_id=(dp, lax.rem(z + step, 8)), device_id_type=MESH
-        )
-    landing[dp] = mine_ref[...]
-    w_buf[0] = own_ref[...]
-    pl.semaphore_wait(barrier, 33)
-
-    def share(step, carry):
-        remote(
-            mine_ref, landing.at[dp], tsem.at[0], tsem.at[1], (lax.rem(dp + step, 32), z)
-        ).start()
-        return carry
-
-    lax.fori_loop(1, 32, share, 0)
-
     def slot_of(place):
         return place[1] * 4 + place[0]
 
-    def sem_of(place, half):
-        return wsem.at[(NEAR + DIAGONAL + FAR).index(place), half]
-
-    def push(source, to, first, count, axis, way):
+    def sem_of(place, half, part):
+        return wsem.at[(NEAR + DIAGONAL + FAR).index(place), half, part]
+
+    def push(source, to, first, count, axis, way, part):
         rows = pl.ds(first * 256, count * 256)
         remote(
-            w_buf.at[slot_of(source), rows], w_buf.at[slot_of(to), rows],
-            wsend.at[axis, way], sem_of(to, first // 2), beside(axis, way),
+            w_buf.at[part, slot_of(source), rows], w_buf.at[part, slot_of(to), rows],
+            wsend.at[axis, way], sem_of(to, first // 2, part), beside(axis, way),
         ).start()
 
-    def landed(place, half):
-        wait_for(w_buf.at[slot_of(place), pl.ds(half * 512, 512)], sem_of(place, half))
-
-    def weights(part):
-        if part == "own":
-            for way in range(2):
-                push((0, 0), (1 + 2 * way, 0), 0, 2, 0, way)
-                push((0, 0), (0, 1 + 2 * way), 2, 2, 1, way)
-        if part == "own b":
-            for way in range(2):
-                push((0, 0), (1 + 2 * way, 0), 2, 2, 0, way)
-        if part in ("side 0", "side 1"):
-            d = 1 if part == "side 0" else 3
-            landed((d, 0), 0)
-            landed((0, d), 1)
-            for way in range(2):
-                push((d, 0), (d, 1 + 2 * way), 0, 2, 1, way)
-                push((0, d), (1 + 2 * way, d), 2, 2, 0, way)
-            if d == 3:
-                push((0, 3), (0, 2), 3, 1, 1, 1)
-        if part == "far b":
-            push((0, 1), (0, 2), 2, 1, 1, 0)
-        if part == "odd":
-            landed((0, 2), 1)
-            for way in range(2):
-                push((0, 2), (1 + 2 * way, 2), 2, 2, 0, way)
+    def landed(place, half, part):
+        wait_for(
+            w_buf.at[part, slot_of(place), pl.ds(half * 512, 512)], sem_of(place, half, part)
+        )
+
+    def weights(stage, part):
+        if stage == "own a":
+            for way in range(2):
+                push((0, 0), (1 + 2 * way, 0), 0, 2, 0, way, part)
+                push((0, 0), (0, 1 + 2 * way), 2, 2, 1, way, part)
+        if stage == "own b":
+            for way in range(2):
+                push((0, 0), (1 + 2 * way, 0), 2, 2, 0, way, part)
+                push((0, 0), (0, 1 + 2 * way), 0, 2, 1, way, part)
+        if stage == "side":
+            for d in (1, 3):
+                landed((d, 0), 0, part)
+                landed((0, d), 1, part)
+                for way in range(2):
+                    push((d, 0), (d, 1 + 2 * way), 0, 2, 1, way, part)
+                    push((0, d), (1 + 2 * way, d), 2, 2, 0, way, part)
+        if stage == "far":
+            for way in range(2):
+                near = 1 + 2 * way
+                landed((near, 0), 1, part)
+                landed((0, near), 0, part)
+                push((near, 0), (2, 0), way, 1, 0, way, part)
+                push((0, near), (0, 2), 2 + way, 1, 1, way, part)
+                push((near, 0), (2, 0), 2 + way, 1, 0, way, part)
+                push((0, near), (0, 2), way, 1, 1, way, part)
+        if stage == "diagonal":
             for dx, dy in DIAGONAL:
-                landed((dx, dy), 0)
-                push((dx, dy), (dx, 2), dy // 2, 1, 1, dy // 2)
-        if part == "own a":
-            for way in range(2):
-                push((0, 0), (0, 1 + 2 * way), 0, 2, 1, way)
-        if part == "even":
-            for way in range(2):
-                landed((1 + 2 * way, 0), 1)
                 for half in range(2):
-                    push((1 + 2 * way, 0), (2, 0), 2 * half + way, 1, 0, way)
-        if part == "odd done":
-            for dx, dy in DIAGONAL:
-                landed((dx, dy), 1)
-                push((dx, dy), (2, dy), 2 + dx // 2, 1, 0, dx // 2)
-            for dx in (1, 3):
-                landed((dx, 2), 1)
-                push((dx, 2), (2, 2), 2 + dx // 2, 1, 0, dx // 2)
-                landed((dx, 2), 0)
-        if part == "even 1":
-            landed((2, 0), 0)
-            for way in range(2):
-                push((2, 0), (2, 1 + 2 * way), 0, 2, 1, way)
-            for way in range(2):
-                landed((0, 1 + 2 * way), 0)
-                push((0, 1 + 2 * way), (0, 2), way, 1, 1, way)
-        if part == "even 2":
-            for way in range(2):
-                landed((2, 1 + 2 * way), 0)
-                push((2, 1 + 2 * way), (2, 2), way, 1, 1, way)
-        if part == "even done":
-            landed((2, 0), 1)
-            landed((0, 2), 0)
-            for way in range(2):
-                landed((2, 1 + 2 * way), 1)
-                landed((2, 2), way)
+                    landed((dx, dy), half, part)
+                push((dx, dy), (dx, 2), dy // 2, 1, 1, dy // 2, part)
+                push((dx, dy), (2, dy), 2 + dx // 2, 1, 0, dx // 2, part)
+        if stage == "far side":
+            landed((2, 0), 0, part)
+            landed((0, 2), 1, part)
+            for way in range(2):
+                push((2, 0), (2, 1 + 2 * way), 0, 2, 1, way, part)
+                push((0, 2), (1 + 2 * way, 2), 2, 2, 0, way, part)
+        if stage == "corner":
+            for way in range(2):
+                side = 1 + 2 * way
+                landed((2, side), 0, part)
+                push((2, side), (2, 2), way, 1, 1, way, part)
+                landed((side, 2), 1, part)
+                push((side, 2), (2, 2), 2 + way, 1, 0, way, part)
+        if stage == "done":
+            landed((2, 0), 1, part)
+            landed((0, 2), 0, part)
+            for way in range(2):
+                side = 1 + 2 * way
+                landed((2, side), 1, part)
+                landed((side, 2), 0, part)
+                landed((2, 2), way, part)
 
     def at_point(point):
-        for part in PLACES[point]:
-            weights(part)
-
+        for stage, part in PLACES[point]:
+            weights(stage, part)
+
+    def same_core(step):
+        return (lax.rem(dp + 2 * step, 32), z)
+
+    def greet(step, carry):
+        pl.semaphore_signal(barrier, inc=1, device_id=same_core(step), device_id_type=MESH)
+        return carry
+
+    lax.fori_loop(1, 16, greet, 0)
+    for other in (partner, (dp, lax.rem(z + 1, 8)), (dp, lax.rem(z + 7, 8))):
+        pl.semaphore_signal(barrier, inc=1, device_id=other, device_id_type=MESH)
+    loads = [
+        pltpu.make_async_copy(source, target, lsem.at[n])
+        for n, (source, target) in enumerate(
+            [
+                (k_hbm, k_ref), (v_hbm, v_ref),
+                (own_ref.at[:, pl.ds(0, 128)], w_buf.at[0, 0]),
+                (own_ref.at[:, pl.ds(128, 128)], w_buf.at[1, 0]), (q_hbm, q_ref),
+                (new_k_hbm, new_k_ref), (new_v_hbm, new_v_ref), (skip_hbm, skip_ref),
+            ]
+        )
+    ]
+    for load in loads:
+        load.start()
+    lane = lax.broadcasted_iota(jnp.int32, (8, 128), 1)
+    numbers = jnp.zeros((8, 128), jnp.int32)
+    for n in range(6):
+        number = parent_ref[n] if n < 2 else extent_ref[n - 2]
+        numbers = jnp.where(lane == n, number, numbers)
+    landing[dp] = numbers
+    loads[2].wait()
+    loads[3].wait()
+    pl.semaphore_wait(barrier, 18)
+
+    beside_me = remote(landing.at[dp], landing.at[dp], tsem.at[3], tsem.at[4], partner)
+    beside_me.start()
+    beside_me.wait_recv()
+    both_cores = landing.at[pl.ds(pl.multiple_of(chip * 2, 2), 2)]
+
+    def share(step, carry):
+        remote(both_cores, both_cores, tsem.at[0], tsem.at[1], same_core(step)).start()
+        return carry
+
+    lax.fori_loop(1, 16, share, 0)
     at_point("start")
-    all_of_them = landing.at[pl.ds(0, 31)]
+
+    all_of_them = landing.at[pl.ds(0, 30)]
     wait_for(all_of_them, tsem.at[1])
     tab_vmem[...] = row_table(landing[:, 0, :], dp)
     to_scalar = pltpu.make_async_copy(tab_vmem, tab, tsem.at[2])
     to_scalar.start()
     to_scalar.wait()
+    for load in loads[:2]:
+        load.wait()
 
     stores = (k_ref, v_ref)
     gathered = (gk, gv)
@@ -301,6 +318,8 @@
                 )
         at_point("relay" if turn == 0 else "own")
     whole = (all_k, all_v)
+    for load in loads[4:]:
+        load.wait()
     for kv in range(2):
         for half in range(2):
             for way in range(2):
@@ -360,22 +379,29 @@
         )
         exchange[-1].start()
         at_point("row%d" % i)
-    weights("odd done")
-
-    def product(d, h, k):
+
+    def product(d, h, part):
         goal = lax.rem(z + d, 8)
-        dx = lax.rem(x - 2 * lax.rem(goal, 2) - k + 4, 4)
         dy = lax.rem(y - goal // 2 + 4, 4)
-        return jnp.dot(a_buf[h], w_buf[dy * 4 + dx], preferred_element_type=jnp.float32)
-
-    def columns_of(round_):
-        return lax.rem(x + 1 + round_, 2)
+        columns = []
+        for k in range(2):
+            dx = lax.rem(x - 2 * lax.rem(goal, 2) - k + 4, 4)
+            columns.append(w_buf[part, dy * 4 + dx])
+        return jnp.dot(
+            a_buf[h], jnp.concatenate(columns, axis=1), preferred_element_type=jnp.float32
+        )
+
+    def finish(round_, owner, value):
+        for k in range(2):
+            columns = pl.ds(pl.multiple_of((2 * k + owner) * 256 + round_ * 128, 128), 128)
+            out_ref[:, columns] = (
+                skip_ref[:, columns].astype(jnp.float32)
+                + value[:, k * 128 : k * 128 + 128].astype(jnp.float32)
+            ).astype(jnp.bfloat16)
 
     def final(round_):
-        k = columns_of(round_)
-
         def total_of(h):
-            value = product(0, h, k)
+            value = product(0, h, round_)
             for way, end in ((0, 3 - h), (1, 2 + h)):
                 for u in range(2):
                     rows = pl.ds(u * 128, 128)
@@ -389,27 +415,24 @@
         remote(
             x_buf.at[0, round_], x_buf.at[1, round_], xsend.at[round_], xrecv.at[round_], partner
         ).start()
-        columns = pl.ds(pl.multiple_of((2 * k + core) * 256, 256), 256)
-        out_ref[:, columns] = (
-            skip_ref[:, columns].astype(jnp.float32) + total_of(core)
-        ).astype(jnp.bfloat16)
+        finish(round_, core, total_of(core))
 
     def step(i, carry):
         round_ = i // 4
         s = lax.rem(i, 4)
-        k = columns_of(round_)
-        for when, part in ((1, "even 1"), (3, "even 2"), (4, "even done")):
-
-            @pl.when(i == when)
-            def _():
-                weights(part)
-
         @pl.when(i == 6)
         def _():
             final(0)
 
         for turn in range(2):
             h = lax.rem(core + turn, 2)
+            for (when, where), (stage, part) in SERVICES.items():
+                if where == turn:
+
+                    @pl.when(i == when)
+                    def _():
+                        weights(stage, part)
+
             if turn == 1:
 
                 @pl.when(i == 0)
@@ -424,7 +447,7 @@
                 @pl.when((d > 0) & (d < 8))
                 def _():
                     place = ((s * 2 + round_) * 2 + way) * 2 + h
-                    t_buf[...] = product(d, h, k)
+                    t_buf[...] = product(d, h, round_)
                     for u in range(2):
                         rows = pl.ds(u * 128, 128)
 
@@ -454,20 +477,17 @@
     lax.fori_loop(0, 8, step, 0)
     final(1)
     for round_ in range(2):
-        k = columns_of(round_)
         wait_for(x_buf.at[1, round_], xrecv.at[round_])
-        columns = pl.ds(pl.multiple_of((2 * k + 1 - core) * 256, 256), 256)
-        out_ref[:, columns] = (
-            skip_ref[:, columns].astype(jnp.float32) + x_buf[1, round_].astype(jnp.float32)
-        ).astype(jnp.bfloat16)
+        finish(round_, 1 - core, x_buf[1, round_])
         wait_for(x_buf.at[0, round_], xsend.at[round_])
     for each in started + exchange:
         each.wait_send()
     wait_for(s_buf.at[pl.ds(0, 28)], ssem)
     wait_for(all_of_them, tsem.at[0])
+    beside_me.wait_send()
     for axis in range(2):
         for way in range(2):
-            wait_for(w_buf.at[pl.ds(0, 15), pl.ds(0, 256)], wsend.at[axis, way])
+            wait_for(w_buf.at[0, pl.ds(0, 15), pl.ds(0, 512)], wsend.at[axis, way])
 
 
 def local(
@@ -481,8 +501,6 @@
     final_projection_matrix,
     skip_stream,
 ):
-    mine = jnp.concatenate([kept_parent, stored_extent])
-    mine = jnp.broadcast_to(jnp.pad(mine, (0, 122))[None], (8, 128))
     vmem = pl.BlockSpec(memory_space=pltpu.VMEM)
     dma = pltpu.SemaphoreType.DMA
     bf16 = jnp.bfloat16
@@ -490,13 +508,20 @@
     return pl.pallas_call(
         layer_kernel,
         out_shape=jax.ShapeDtypeStruct(skip_stream.shape, skip_stream.dtype),
-        in_specs=[vmem] * 8,
+        in_specs=[pl.BlockSpec(memory_space=pltpu.SMEM)] * 2
+        + [pl.BlockSpec(memory_space=pl.ANY)] * 7,
         out_specs=vmem,
         scratch_shapes=[
             pltpu.VMEM((32, 8, 128), jnp.int32),
             pltpu.VMEM((32, 128), jnp.int32),
             pltpu.SMEM((32, 128), jnp.int32),
-            pltpu.VMEM((16, 1024, 256), bf16),
+            pltpu.VMEM((2, 16, 1024, 128), bf16),
+            pltpu.VMEM(question_vectors.shape, bf16),
+            pltpu.VMEM(arriving_lookup_vectors.shape, bf16),
+            pltpu.VMEM(arriving_content_vectors.shape, bf16),
+            pltpu.VMEM(earlier_lookup_store.shape, bf16),
+            pltpu.VMEM(earlier_content_store.shape, bf16),
+            pltpu.VMEM(skip_stream.shape, bf16),
             pltpu.VMEM((2, 2, 512, 128), bf16),
             pltpu.VMEM((4, 4) + item, bf16),
             pltpu.VMEM((4, 4) + item, bf16),
@@ -513,7 +538,7 @@
             pltpu.VMEM((4, 2, 2, 2, 256, 256), bf16),
             pltpu.VMEM((256, 256), jnp.float32),
             pltpu.VMEM((2, 2, 256, 256), bf16),
-            dma((3,)), dma((15, 2)), dma((2, 2)),
+            dma((5,)), dma((8,)), dma((15, 2, 2)), dma((2, 2)),
             dma((2,)), dma((2,)),
             dma((2, 2, 2)), dma((2, 2, 2)),
             dma((2, 2)), dma((2, 2)),
@@ -523,13 +548,14 @@
             dma((4, 2, 2, 2, 2)), dma, dma((2, 2)), dma((2,)), dma((2,)),
         ],
         compiler_params=pltpu.CompilerParams(
-            collective_id=1, has_side_effects=True, vmem_limit_bytes=56 * 1024 * 1024
+            collective_id=1, has_side_effects=True, vmem_limit_bytes=60 * 1024 * 1024
         ),
         cost_estimate=pl.CostEstimate(
             flops=10 << 30, bytes_accessed=8 << 20, transcendentals=2 << 20
         ),
     )(
-        mine,
+        kept_parent,
+        stored_extent,
         question_vectors,
         arriving_lookup_vectors,
         arriving_content_vectors,

time: 111 us -> 107 us (0.964)
  Pallas kernels: 108 us -> 105 us
    pallas_call x1, Pallas kernels: 108 us -> 105 us  [local(): pl.pallas_call(layer_kernel, out_shape=jax.ShapeDtypeStruct(skip_stream.s...]
where the time goes in v6:
time: 107 us
  Pallas kernels  105 us (98%)
  local copies, waits for them, and re-layouts  1.87 us (2%)
    pallas_call x1, Pallas kernels, local(): pl.pallas_call(layer_kernel, out_shape=jax.ShapeDtypeStruct(skip_stream.s...  105 us

profile of v6, /device:TPU:1, one launch (start us, length us, event | category | flops | bytes accessed | tf_op | source)
XLA Modules:
  0.0 107.0 jit_solution(10143186665069981595)
XLA Ops:
  0.0 105.2 %shard_map.91 = bf16[256,1024]{1,0:T(8,128)(2,1)} custom-call(s32[2]{0:T(128)} %parent_ref.1, s32[4]{0:T(128)} %extent_ref.1, bf16[2,128,1024]{2,1,0:T(8,128)(2,1)} %q_hbm.1, bf16[2,128,128]{2,1,0:T(8,128)(2,1)} %new_k_hbm.1, bf16[2,128,128]{2,1,0:T(8,128)(2,1)} %new_v_hbm.1, bf16[4,512,128]{2,1,0:T(8,128)(2,1)} %k_hbm.1, bf16[4,512,128]{2,1,0:T(8,128)(2,1)} %v_hbm.1, ...), custom_call_target="tpu_custom_call" | custom-call | flops 10737418240 | bytes 8388608 | tf_op jit(solution)/shard_map/pallas_call | solution.py:508
  105.2 1.9 %copy.11 = bf16[256,1024]{1,0:T(8,128)(2,1)} copy(bf16[256,1024]{1,0:T(8,128)(2,1)} %shard_map.91) | data formatting | bytes 1048576

commit v7 on v6

--- a/solution.py
+++ b/solution.py
@@ -78,7 +78,7 @@
 NEAR = [(1, 0), (3, 0), (0, 1), (0, 3)]
 DIAGONAL = [(1, 1), (1, 3), (3, 1), (3, 3)]
 FAR = [(2, 0), (0, 2), (2, 1), (2, 3), (1, 2), (3, 2), (2, 2)]
-PLACES = {'start': [('own a', 0), ('own b', 0)], 'gather': [], 'forward': [('side', 0)], 'select': [('far', 0)], 'relay': [], 'own': [('diagonal', 0), ('far side', 0), ('own a', 1)], 'swap': [('corner', 0)], 'row0': [('own b', 1)], 'row1': [('done', 0)]}
+PLACES = {'start': [('own a', 0), ('own b', 0)], 'gather': [], 'forward': [('far', 0)], 'select': [('side', 0)], 'relay': [], 'own': [('far side', 0), ('diagonal', 0)], 'swap': [('corner', 0)], 'row0': [('own a', 1), ('own b', 1)], 'row1': [('done', 0)]}
 SERVICES = {
     (0, 1): ("side", 1),
     (1, 0): ("far", 1),
@@ -132,14 +132,18 @@
                 push((0, 0), (0, 1 + 2 * way), 0, 2, 1, way, part)
         if stage == "side":
             for d in (1, 3):
-                landed((d, 0), 0, part)
-                landed((0, d), 1, part)
+                if part == 1:
+                    landed((d, 0), 0, part)
+                    landed((0, d), 1, part)
                 for way in range(2):
                     push((d, 0), (d, 1 + 2 * way), 0, 2, 1, way, part)
                     push((0, d), (1 + 2 * way, d), 2, 2, 0, way, part)
         if stage == "far":
             for way in range(2):
                 near = 1 + 2 * way
+                if part == 0:
+                    landed((near, 0), 0, part)
+                    landed((0, near), 1, part)
                 landed((near, 0), 1, part)
                 landed((0, near), 0, part)
                 push((near, 0), (2, 0), way, 1, 0, way, part)

time: 107 us -> 105 us (0.981)
  Pallas kernels: 105 us -> 103 us
    pallas_call x1, Pallas kernels: 105 us -> 103 us  [local(): pl.pallas_call(layer_kernel, out_shape=jax.ShapeDtypeStruct(skip_stream.s...]
where the time goes in v7:
time: 105 us
  Pallas kernels  103 us (98%)
  local copies, waits for them, and re-layouts  1.87 us (2%)
    pallas_call x1, Pallas kernels, local(): pl.pallas_call(layer_kernel, out_shape=jax.ShapeDtypeStruct(skip_stream.s...  103 us

profile of v7, /device:TPU:1, one launch (start us, length us, event | category | flops | bytes accessed | tf_op | source)
XLA Modules:
  0.0 104.7 jit_solution(15699870747282047569)
XLA Ops:
  0.0 102.9 %shard_map.91 = bf16[256,1024]{1,0:T(8,128)(2,1)} custom-call(s32[2]{0:T(128)} %parent_ref.1, s32[4]{0:T(128)} %extent_ref.1, bf16[2,128,1024]{2,1,0:T(8,128)(2,1)} %q_hbm.1, bf16[2,128,128]{2,1,0:T(8,128)(2,1)} %new_k_hbm.1, bf16[2,128,128]{2,1,0:T(8,128)(2,1)} %new_v_hbm.1, bf16[4,512,128]{2,1,0:T(8,128)(2,1)} %k_hbm.1, bf16[4,512,128]{2,1,0:T(8,128)(2,1)} %v_hbm.1, ...), custom_call_target="tpu_custom_call" | custom-call | flops 10737418240 | bytes 8388608 | tf_op jit(solution)/shard_map/pallas_call | solution.py:512
  102.9 1.9 %copy.11 = bf16[256,1024]{1,0:T(8,128)(2,1)} copy(bf16[256,1024]{1,0:T(8,128)(2,1)} %shard_map.91) | data formatting | bytes 1048576

commit v8 on v7

--- a/solution.py
+++ b/solution.py
@@ -90,8 +90,8 @@
 
 
 def layer_kernel(
-    parent_ref, extent_ref, q_hbm, new_k_hbm, new_v_hbm, k_hbm, v_hbm, own_ref, skip_hbm, out_ref,
-    landing, tab_vmem, tab, w_buf, q_ref, new_k_ref, new_v_ref, k_ref, v_ref, skip_ref,
+    parent_hbm, extent_hbm, q_hbm, new_k_hbm, new_v_hbm, k_hbm, v_hbm, own_ref, skip_hbm, out_hbm,
+    landing, tab_vmem, tab, w_buf, q_ref, new_k_ref, new_v_ref, k_ref, v_ref, skip_ref, parent_ref, extent_ref, out_ref, osem,
     picked, gk, gv, s1, r1, s2, r2, fin, xin, all_k, all_v,
     a_buf, s_buf, r_buf, t_buf, x_buf,
     tsem, lsem, wsem, wsend,
@@ -192,6 +192,12 @@
     lax.fori_loop(1, 16, greet, 0)
     for other in (partner, (dp, lax.rem(z + 1, 8)), (dp, lax.rem(z + 7, 8))):
         pl.semaphore_signal(barrier, inc=1, device_id=other, device_id_type=MESH)
+    numbers_in = [
+        pltpu.make_async_copy(parent_hbm, parent_ref, lsem.at[8]),
+        pltpu.make_async_copy(extent_hbm, extent_ref, lsem.at[9]),
+    ]
+    for load in numbers_in:
+        load.start()
     loads = [
         pltpu.make_async_copy(source, target, lsem.at[n])
         for n, (source, target) in enumerate(
@@ -205,6 +211,8 @@
     ]
     for load in loads:
         load.start()
+    for load in numbers_in:
+        load.wait()
     lane = lax.broadcasted_iota(jnp.int32, (8, 128), 1)
     numbers = jnp.zeros((8, 128), jnp.int32)
     for n in range(6):
@@ -402,6 +410,9 @@
                 skip_ref[:, columns].astype(jnp.float32)
                 + value[:, k * 128 : k * 128 + 128].astype(jnp.float32)
             ).astype(jnp.bfloat16)
+            pltpu.make_async_copy(
+                out_ref.at[:, columns], out_hbm.at[:, columns], osem.at[round_, owner, k]
+            ).start()
 
     def final(round_):
         def total_of(h):
@@ -479,11 +490,22 @@
         return carry
 
     lax.fori_loop(0, 8, step, 0)
-    final(1)
-    for round_ in range(2):
+
+    def theirs(round_):
         wait_for(x_buf.at[1, round_], xrecv.at[round_])
         finish(round_, 1 - core, x_buf[1, round_])
         wait_for(x_buf.at[0, round_], xsend.at[round_])
+
+    theirs(0)
+    final(1)
+    theirs(1)
+    for round_ in range(2):
+        for owner in range(2):
+            for k in range(2):
+                piece = pl.ds((2 * k + owner) * 256 + round_ * 128, 128)
+                pltpu.make_async_copy(
+                    out_ref.at[:, piece], out_hbm.at[:, piece], osem.at[round_, owner, k]
+                ).wait()
     for each in started + exchange:
         each.wait_send()
     wait_for(s_buf.at[pl.ds(0, 28)], ssem)
@@ -505,16 +527,14 @@
     final_projection_matrix,
     skip_stream,
 ):
-    vmem = pl.BlockSpec(memory_space=pltpu.VMEM)
     dma = pltpu.SemaphoreType.DMA
     bf16 = jnp.bfloat16
     item = (256, 128)
     return pl.pallas_call(
         layer_kernel,
         out_shape=jax.ShapeDtypeStruct(skip_stream.shape, skip_stream.dtype),
-        in_specs=[pl.BlockSpec(memory_space=pltpu.SMEM)] * 2
-        + [pl.BlockSpec(memory_space=pl.ANY)] * 7,
-        out_specs=vmem,
+        in_specs=[pl.BlockSpec(memory_space=pl.ANY)] * 9,
+        out_specs=pl.BlockSpec(memory_space=pl.ANY),
         scratch_shapes=[
             pltpu.VMEM((32, 8, 128), jnp.int32),
             pltpu.VMEM((32, 128), jnp.int32),
@@ -526,6 +546,10 @@
             pltpu.VMEM(earlier_lookup_store.shape, bf16),
             pltpu.VMEM(earlier_content_store.shape, bf16),
             pltpu.VMEM(skip_stream.shape, bf16),
+            pltpu.SMEM(kept_parent.shape, jnp.int32),
+            pltpu.SMEM(stored_extent.shape, jnp.int32),
+            pltpu.VMEM(skip_stream.shape, bf16),
+            dma((2, 2, 2)),
             pltpu.VMEM((2, 2, 512, 128), bf16),
             pltpu.VMEM((4, 4) + item, bf16),
             pltpu.VMEM((4, 4) + item, bf16),
@@ -542,7 +566,7 @@
             pltpu.VMEM((4, 2, 2, 2, 256, 256), bf16),
             pltpu.VMEM((256, 256), jnp.float32),
             pltpu.VMEM((2, 2, 256, 256), bf16),
-            dma((5,)), dma((8,)), dma((15, 2, 2)), dma((2, 2)),
+            dma((5,)), dma((10,)), dma((15, 2, 2)), dma((2, 2)),
             dma((2,)), dma((2,)),
             dma((2, 2, 2)), dma((2, 2, 2)),
             dma((2, 2)), dma((2, 2)),

time: 105 us -> 105 us (level)
  no operation moved by 1% of the time
where the time goes in v8:
time: 105 us; the launch traced here: 104 us
  Pallas kernels  102 us (97%)
  local copies, waits for them, and re-layouts  1.87 us (2%)
    pallas_call x1, Pallas kernels, local(): pl.pallas_call(layer_kernel, out_shape=jax.ShapeDtypeStruct(skip_stream.s...  102 us

profile of v8, /device:TPU:1, one launch (start us, length us, event | category | flops | bytes accessed | tf_op | source)
XLA Modules:
  0.0 103.9 jit_solution(15561564251949542595)
XLA Ops:
  0.0 102.0 %shard_map.91 = bf16[256,1024]{1,0:T(8,128)(2,1)} custom-call(s32[2]{0:T(128)} %parent_hbm.1, s32[4]{0:T(128)} %extent_hbm.1, bf16[2,128,1024]{2,1,0:T(8,128)(2,1)} %q_hbm.1, bf16[2,128,128]{2,1,0:T(8,128)(2,1)} %new_k_hbm.1, bf16[2,128,128]{2,1,0:T(8,128)(2,1)} %new_v_hbm.1, bf16[4,512,128]{2,1,0:T(8,128)(2,1)} %k_hbm.1, bf16[4,512,128]{2,1,0:T(8,128)(2,1)} %v_hbm.1, ...), custom_call_target="tpu_custom_call" | custom-call | flops 10737418240 | bytes 8388608 | tf_op jit(solution)/shard_map/pallas_call | solution.py:533
  102.0 1.9 %copy.11 = bf16[256,1024]{1,0:T(8,128)(2,1)} copy(bf16[256,1024]{1,0:T(8,128)(2,1)} %shard_map.91) | data formatting | bytes 1048576

commit v9 on v8

--- a/solution.py
+++ b/solution.py
@@ -189,7 +189,8 @@
         pl.semaphore_signal(barrier, inc=1, device_id=same_core(step), device_id_type=MESH)
         return carry
 
-    lax.fori_loop(1, 16, greet, 0)
+    for step in range(1, 16):
+        greet(step, 0)
     for other in (partner, (dp, lax.rem(z + 1, 8)), (dp, lax.rem(z + 7, 8))):
         pl.semaphore_signal(barrier, inc=1, device_id=other, device_id_type=MESH)
     numbers_in = [
@@ -232,7 +233,8 @@
         remote(both_cores, both_cores, tsem.at[0], tsem.at[1], same_core(step)).start()
         return carry
 
-    lax.fori_loop(1, 16, share, 0)
+    for step in range(1, 16):
+        share(step, 0)
     at_point("start")
 
     all_of_them = landing.at[pl.ds(0, 30)]
@@ -440,7 +442,7 @@
             final(0)
 
         for turn in range(2):
-            h = lax.rem(core + turn, 2)
+            h = lax.rem(core + turn + round_, 2)
             for (when, where), (stage, part) in SERVICES.items():
                 if where == turn:
 

time: 105 us -> 104 us (level)
  no operation moved by 1% of the time
where the time goes in v9:
time: 104 us; the launch traced here: 103 us
  Pallas kernels  101 us (97%)
  local copies, waits for them, and re-layouts  1.87 us (2%)
    pallas_call x1, Pallas kernels, local(): pl.pallas_call(layer_kernel, out_shape=jax.ShapeDtypeStruct(skip_stream.s...  101 us

profile of v9, /device:TPU:1, one launch (start us, length us, event | category | flops | bytes accessed | tf_op | source)
XLA Modules:
  0.0 103.0 jit_solution(14726676891690505237)
XLA Ops:
  0.0 101.1 %shard_map.91 = bf16[256,1024]{1,0:T(8,128)(2,1)} custom-call(s32[2]{0:T(128)} %parent_hbm.1, s32[4]{0:T(128)} %extent_hbm.1, bf16[2,128,1024]{2,1,0:T(8,128)(2,1)} %q_hbm.1, bf16[2,128,128]{2,1,0:T(8,128)(2,1)} %new_k_hbm.1, bf16[2,128,128]{2,1,0:T(8,128)(2,1)} %new_v_hbm.1, bf16[4,512,128]{2,1,0:T(8,128)(2,1)} %k_hbm.1, bf16[4,512,128]{2,1,0:T(8,128)(2,1)} %v_hbm.1, ...), custom_call_target="tpu_custom_call" | custom-call | flops 10737418240 | bytes 8388608 | tf_op jit(solution)/shard_map/pallas_call | solution.py:535
  101.1 1.9 %copy.11 = bf16[256,1024]{1,0:T(8,128)(2,1)} copy(bf16[256,1024]{1,0:T(8,128)(2,1)} %shard_map.91) | data formatting | bytes 1048576

commit v10 on v8

--- a/solution.py
+++ b/solution.py
@@ -37,6 +37,16 @@
 
 def wait_for(ref, sem):
     pltpu.make_async_copy(ref, ref, sem).wait()
+
+
+def row_length(table, dp, i):
+    lane = lax.broadcasted_iota(jnp.int32, (32, 128), 1)
+    line = lax.broadcasted_iota(jnp.int32, (32, 128), 0)
+    wanted = jnp.where((line == dp) & (lane == i), table, 0)
+    wanted = jnp.sum(jnp.sum(wanted, axis=0, keepdims=True), axis=1, keepdims=True)
+    found = (lane >= 2) & (lane < 6) & (line * 4 + lane - 2 == wanted)
+    found = jnp.sum(jnp.where(found, table, 0), axis=0, keepdims=True)
+    return jnp.sum(found, axis=1, keepdims=True)
 
 
 def row_table(table, dp):
@@ -65,12 +75,6 @@
         slot = jnp.bitwise_and(parents[i], 3)
         low = jnp.minimum(low, jnp.min(jnp.where(here, slot, 9), axis=0, keepdims=True))
         high = jnp.maximum(high, jnp.max(jnp.where(here, slot, -1), axis=0, keepdims=True))
-        wanted = jnp.sum(jnp.where(line[:, :1] == dp, parents[i], 0), axis=0, keepdims=True)
-        found = (lane >= 2) & (lane < 6) & (line * 4 + lane - 2 == wanted)
-        extent = jnp.sum(
-            jnp.sum(jnp.where(found, table, 0), axis=0, keepdims=True), axis=1, keepdims=True
-        )
-        result = jnp.where(lane == 4 + i, extent, result)
     result = jnp.where(lane == 2, jnp.minimum(low, 3), result)
     return jnp.where(lane == 3, jnp.maximum(high, 0), result)
 
@@ -359,7 +363,7 @@
     for i in range(2):
         position = lax.broadcasted_iota(jnp.int32, (2 * STRETCH, span), 1)
         token = lax.rem(lax.broadcasted_iota(jnp.int32, (2 * STRETCH, span), 0), STRETCH)
-        bound = jnp.where(position < CACHE, tab[0, 4 + i], token + CACHE + 1)
+        bound = jnp.where(position < CACHE, row_length(landing[:, 0, :], dp, i), token + CACHE + 1)
         penalty = jnp.where(position < bound, 0.0, -1e30)
         tokens = pl.ds(i * STRETCH, STRETCH)
 

time: 105 us -> 105 us (level)
  no operation moved by 1% of the time
where the time goes in v10:
time: 105 us
  Pallas kernels  103 us (98%)
  local copies, waits for them, and re-layouts  1.87 us (2%)
    pallas_call x1, Pallas kernels, local(): pl.pallas_call(layer_kernel, out_shape=jax.ShapeDtypeStruct(skip_stream.s...  103 us

profile of v10, /device:TPU:1, one launch (start us, length us, event | category | flops | bytes accessed | tf_op | source)
XLA Modules:
  0.0 104.9 jit_solution(15088256223281972286)
XLA Ops:
  0.0 103.0 %shard_map.91 = bf16[256,1024]{1,0:T(8,128)(2,1)} custom-call(s32[2]{0:T(128)} %parent_hbm.1, s32[4]{0:T(128)} %extent_hbm.1, bf16[2,128,1024]{2,1,0:T(8,128)(2,1)} %q_hbm.1, bf16[2,128,128]{2,1,0:T(8,128)(2,1)} %new_k_hbm.1, bf16[2,128,128]{2,1,0:T(8,128)(2,1)} %new_v_hbm.1, bf16[4,512,128]{2,1,0:T(8,128)(2,1)} %k_hbm.1, bf16[4,512,128]{2,1,0:T(8,128)(2,1)} %v_hbm.1, ...), custom_call_target="tpu_custom_call" | custom-call | flops 10737418240 | bytes 8388608 | tf_op jit(solution)/shard_map/pallas_call | solution.py:537
  103.0 1.9 %copy.11 = bf16[256,1024]{1,0:T(8,128)(2,1)} copy(bf16[256,1024]{1,0:T(8,128)(2,1)} %shard_map.91) | data formatting | bytes 1048576
